TPU v7x, 256 devices: a whole 4x4x8 slice. The times are simulated.
256 devices in a mesh: seq: 64 (over z, y, core), res: 4 (over x).
Axes of the slice: x: 4, y: 4, z: 8, core: 2. Of those that a mesh axis runs over, the one named last changes fastest.
Arguments:
- alignment_embedding: bfloat16 [256, 512, 768], P('seq', 'res'), may hold values from -6 to 6
- horizontal_scaling_factor: float32 [768], replicated, may hold values from 0.25 to 1.75
- horizontal_asking_matrix: bfloat16 [768, 768], replicated, may hold values from -4 to 4
- horizontal_lookup_matrix: bfloat16 [768, 768], replicated, may hold values from -4 to 4
- horizontal_content_matrix: bfloat16 [768, 768], replicated, may hold values from -0.21875 to 0.21875
- horizontal_mixing_matrix: bfloat16 [768, 768], replicated, may hold values from -0.21875 to 0.21875
- vertical_scaling_factor: float32 [768], replicated, may hold values from 0.25 to 1.75
- vertical_asking_matrix: bfloat16 [768, 768], replicated, may hold values from -4 to 4
- vertical_lookup_matrix: bfloat16 [768, 768], replicated, may hold values from -4 to 4
- vertical_content_matrix: bfloat16 [768, 768], replicated, may hold values from -0.21875 to 0.21875
- vertical_mixing_matrix: bfloat16 [768, 768], replicated, may hold values from -0.21875 to 0.21875
Outputs:
- result: bfloat16 [256, 512, 768], P('seq', 'res')
All inputs are finite; a program needn't handle non-finite values.
Results may differ from a plain program's by a relative error of at most 0.009.
Values may be sent and summed in bfloat16 or wider, within the bound.
A program may use at most 64 MiB of HBM per device.

v0:
```python
import math

import jax
import jax.numpy as jnp
from jax import lax
from jax.sharding import PartitionSpec as P

HEADS = 12


def standardize_activations(values, gain):
    wide = values.astype(jnp.float32)
    center = wide - jnp.mean(wide, axis=-1, keepdims=True)
    spread = jnp.mean(center * center, axis=-1, keepdims=True)
    return (center * lax.rsqrt(spread + 1e-05) * gain).astype(jnp.bfloat16)


def project(standardized_hidden, weight):
    embedding_dimension = weight.shape[0]
    return jnp.dot(
        standardized_hidden.reshape(-1, embedding_dimension),
        weight,
        preferred_element_type=jnp.float32,
    ).astype(jnp.bfloat16)


def on_device(
    alignment_embedding,
    horizontal_scaling_factor,
    horizontal_asking_matrix,
    horizontal_lookup_matrix,
    horizontal_content_matrix,
    horizontal_mixing_matrix,
    vertical_scaling_factor,
    vertical_asking_matrix,
    vertical_lookup_matrix,
    vertical_content_matrix,
    vertical_mixing_matrix,
):
    device_chain_total, device_site_total, embedding_dimension = alignment_embedding.shape
    head_size = embedding_dimension // HEADS
    total_seqs = device_chain_total * lax.axis_size("seq")
    standardized_hidden = standardize_activations(alignment_embedding, horizontal_scaling_factor)
    row_q = project(standardized_hidden, horizontal_asking_matrix).reshape(
        device_chain_total, device_site_total, HEADS, head_size
    )
    row_k = project(standardized_hidden, horizontal_lookup_matrix).reshape(
        device_chain_total, device_site_total, HEADS, head_size
    )
    row_v = project(standardized_hidden, horizontal_content_matrix).reshape(
        device_chain_total, device_site_total, HEADS, head_size
    )
    factor = 1.0 / (math.sqrt(head_size) * math.sqrt(total_seqs))
    all_keys, all_values = (
        lax.all_gather(row_k, "res", axis=1, tiled=True),
        lax.all_gather(row_v, "res", axis=1, tiled=True),
    )
    partial_logits = (
        jnp.einsum("sihe,sjhe->hij", row_q, all_keys, preferred_element_type=jnp.float32) * factor
    )
    tied = lax.psum(partial_logits, "seq")
    row_prob = jax.nn.softmax(tied, axis=-1).astype(jnp.bfloat16)
    row_attended = jnp.einsum(
        "hij,sjhe->sihe", row_prob, all_values, preferred_element_type=jnp.float32
    )
    row_attended = row_attended.astype(jnp.bfloat16).reshape(-1, embedding_dimension)
    residual_increment = jnp.dot(
        row_attended, horizontal_mixing_matrix, preferred_element_type=jnp.float32
    ).reshape(alignment_embedding.shape)
    hidden_post_horizontal = (alignment_embedding.astype(jnp.float32) + residual_increment).astype(
        jnp.bfloat16
    )
    groups = lax.axis_size("seq")
    columns = device_site_total // groups
    grouped = hidden_post_horizontal.reshape(
        device_chain_total, groups, columns, embedding_dimension
    )
    block = lax.all_to_all(grouped, "seq", split_axis=1, concat_axis=0, tiled=True)
    rows_all, single, count, _ = block.shape
    col_normed = standardize_activations(block, vertical_scaling_factor)
    col_q = project(col_normed, vertical_asking_matrix).reshape(rows_all, count, HEADS, head_size)
    col_k = project(col_normed, vertical_lookup_matrix).reshape(rows_all, count, HEADS, head_size)
    col_v = project(col_normed, vertical_content_matrix).reshape(rows_all, count, HEADS, head_size)
    scores = jnp.einsum("sche,tche->chst", col_q, col_k, preferred_element_type=jnp.float32) * (
        1.0 / math.sqrt(head_size)
    )
    col_prob = jax.nn.softmax(scores, axis=-1).astype(jnp.bfloat16)
    col_mixed = jnp.einsum(
        "chst,tche->sche", col_prob, col_v, preferred_element_type=jnp.float32
    ).astype(jnp.bfloat16)
    change = jnp.dot(
        col_mixed.reshape(-1, embedding_dimension),
        vertical_mixing_matrix,
        preferred_element_type=jnp.float32,
    ).reshape(block.shape)
    regrouped = (block.astype(jnp.float32) + change).astype(jnp.bfloat16)
    restored = lax.all_to_all(regrouped, "seq", split_axis=0, concat_axis=1, tiled=True)
    return restored.reshape(device_chain_total, device_site_total, embedding_dimension)


def solution(mesh):
    in_specs = (P("seq", "res", None), P(), P(), P(), P(), P(), P(), P(), P(), P(), P())
    out_specs = P("seq", "res", None)
    return jax.shard_map(
        on_device, mesh=mesh, in_specs=in_specs, out_specs=out_specs, check_vma=False
    )
```

profile of v0, /device:TPU:1, one launch (start us, length us, event | category | flops | bytes accessed | tf_op | source)
XLA Modules:
  0.0 421.8 jit_solution(9793978674634448692)
XLA Ops:
  6.5 1.4 convert_reduce_fusion
  8.0 1.5 fusion.9
  11.1 1.1 copy.42
  12.3 2.0 convolution_convert_fusion.4
  14.8 46.2 %all-gather.5.cloned.1.call-done = bf16[4,512,12,64]{1,3,0,2:T(8,128)(2,1)} async-done(((bf16[4,128,12,64]{1,3,0,2:T(8,128)(2,1)}), bf16[4,512,12,64]{1,3,0,2:T(8,128)(2,1)}) %all-gather.5.cloned.1.call-update) | async-done | bytes 3145744 | tf_op jit(solution)/shard_map/all_gather | solution.py:55
  61.0 4.2 bitcast_multiply_fusion
  65.3 1.2 copy-done.7
  67.8 1.1 copy.39
  68.9 189.3 %all-reduce.2.cloned.1.call-done = f32[12,128,512]{2,1,0:T(8,128)} async-done(((f32[12,128,512]{2,1,0:T(8,128)}), f32[12,128,512]{2,1,0:T(8,128)}) %all-reduce.2.cloned.1.call-update) | async-done | bytes 3145744 | tf_op jit(solution)/shard_map/psum | solution.py:61
  258.2 3.6 fusion.36
  261.8 43.6 %all-gather.3.cloned.1.call-done = bf16[4,512,12,64]{1,3,0,2:T(8,128)(2,1)} async-done(((bf16[4,128,12,64]{1,3,0,2:T(8,128)(2,1)}), bf16[4,512,12,64]{1,3,0,2:T(8,128)(2,1)}) %all-gather.3.cloned.1.call-update) | async-done | bytes 3145744 | tf_op jit(solution)/shard_map/all_gather | solution.py:56
  305.4 6.7 %fusion.26 = bf16[4,128,12,64]{1,3,0,2:T(8,128)(2,1)S(1)} fusion(bf16[4,512,12,64]{1,3,0,2:T(8,128)(2,1)} %all-gather.3.cloned.1.call-done, f32[12,128]{1,0:T(8,128)S(1)} %fusion.36, f32[12,128,512]{2,1,0:T(8,128)} %all-reduce.2.cloned.1.call-done), kind=kOutput, calls=%fused_computation.38 | convolution fusion | flops 405407744 | bytes 7084032 | tf_op jit(solution)/shard_map/hij,sjhe->sihe/dot_general | solution.py:63
  312.2 1.2 copy-done.4
  313.4 0.8 fusion.12
  315.1 34.1 %all_to_all.24 = bf16[4,64,2,768]{3,2,0,1:T(2,128)(2,1)S(1)} all-to-all(bf16[4,64,2,768]{3,2,0,1:T(2,128)(2,1)S(1)} %copy.46), channel_id=1, replica_groups=mesh['seq'=64,'res'=4] {'seq'}, dimensions={1} | all-to-all | bytes 1572864 | tf_op jit(solution)/shard_map/all_to_all | solution.py:78
  350.2 1.6 multiply_reduce_fusion.1
  352.0 2.0 bitcast_convert_fusion
  354.0 1.1 reshape.140
  355.4 1.0 copy-done.8
  356.4 1.7 convolution_convert_fusion.1
  358.0 2.7 reshape.136
  360.8 2.9 convolution_convert_fusion
  363.7 3.8 reshape.137
  367.5 2.9 fusion.17
  370.4 4.2 %fusion.37 = (f32[2,12,256]{2,1,0:T(8,128)S(1)}, f32[2,12,256,256]{2,3,1,0:T(8,128)}) fusion(f32[2,12,256,256]{2,3,1,0:T(8,128)S(1)} %fusion.17), kind=kOutput, calls=%fused_computation.53 | output fusion | flops 6291711 | bytes 12607488 | tf_op jit(solution)/shard_map/sub | solution.py:87
  374.6 1.7 convolution_convert_fusion.2
  376.3 2.7 reshape.135
  379.0 4.1 fusion.23
  383.1 0.8 fusion.29
  383.9 0.8 copy.53
  384.8 28.8 %all_to_all.25 = bf16[256,1,2,768]{3,2,1,0:T(2,128)(2,1)S(1)} all-to-all(bf16[256,1,2,768]{3,2,1,0:T(2,128)(2,1)S(1)} %copy.53), channel_id=1, replica_groups=mesh['seq'=64,'res'=4] {'seq'}, dimensions={0} | all-to-all | bytes 1572864 | tf_op jit(solution)/shard_map/all_to_all | solution.py:97
  414.1 1.2 reshape.138
  (46 shorter events, 6.3 us)
Async XLA Ops:
  6.5 3.3 copy-start
  6.5 3.0 copy-start.2
  6.5 3.0 copy-start.5
  6.5 54.5 %all-gather.5.cloned.1.call-start = ((), (), s32[]{:S(2)}) async-start(), calls=%async_computation.3 | async-start | bytes 3932160 | tf_op jit(solution)/shard_map/all_gather | solution.py:55
  12.2 246.0 %all-reduce.2.cloned.1.call-start = ((), (), s32[]{:S(2)}) async-start(), calls=%async_computation.4 | async-start | bytes 6291456 | tf_op jit(solution)/shard_map/psum | solution.py:61
  65.2 1.3 copy-start.7
  65.3 240.1 %all-gather.3.cloned.1.call-start = ((), (), s32[]{:S(2)}) async-start(), calls=%async_computation.2 | async-start | bytes 3932160 | tf_op jit(solution)/shard_map/all_gather | solution.py:56
  312.1 1.3 copy-start.4
  354.0 1.1 copy-start.6
  355.1 1.3 copy-start.8
  370.3 4.3 %copy-start.9 = (bf16[768,768]{1,0:T(8,128)(2,1)S(1)}, bf16[768,768]{1,0:T(8,128)(2,1)}, u32[]{:S(2)}) copy-start(bf16[768,768]{1,0:T(8,128)(2,1)} %param.20) | copy-start | bytes 3538948
  379.0 4.1 copy-start.3
  379.0 4.1 copy-start.10
  413.6 1.7 copy-start.1
Sparse Core Ops, SparseCore 0:
  12.3 48.6 all-gather.4
  65.4 192.7 all-reduce.1
  260.2 45.2 all-gather.2
where the time goes:
time: 422 us
  waiting for transfers between devices  279 us (66%)
  blocking collectives  62.9 us (15%)
  matrix products  29.3 us (7%)
  local copies, waits for them, and re-layouts  21 us (5%)
  other arithmetic  15.8 us (4%)
  between operations  13.4 us (3%)
    psum x1, waiting for transfers between devices, on_device(): tied = lax.psum(partial_logits, 'seq')  189 us
    all_gather x1, waiting for transfers between devices, on_device(): lax.all_gather(row_k, 'res', axis=1, tiled=True)  46.2 us
    all_gather x1, waiting for transfers between devices, on_device(): lax.all_gather(row_v, 'res', axis=1, tiled=True)  43.6 us
    all_to_all x1, blocking collectives, on_device(): lax.all_to_all(grouped, 'seq', split_axis=1, concat_axis=0, tiled=True)  34.1 us
    all_to_all x1, blocking collectives, on_device(): lax.all_to_all(regrouped, 'seq', split_axis=0, concat_axis=1, tiled=True)  28.8 us
    dot_general x6, matrix products, project(): jnp.dot(standardized_hidden.reshape(-1, embedding_dimension), weight, pre...  9.87 us
  transfers between devices with their start and end apart: 3, of which 3 were waited for; matrix products, arithmetic and copies ran while one was open for 2% of the time, Pallas kernels for 0%

commit v1 on v0

v1 whole, which is shorter than its diff:
```python
import functools
import math

import jax
import jax.numpy as jnp
from jax import lax
from jax.experimental import pallas as pl
from jax.experimental.pallas import tpu as pltpu
from jax.sharding import PartitionSpec as P

MESH = pl.DeviceIdType.MESH
HEADS = 12
HEAD = 64
WIDTH = HEADS * HEAD
LANES = 128
SLABS = WIDTH // LANES
BF = jnp.bfloat16
F32 = jnp.float32
NT = (((1,), (1,)), ((), ()))


class Dims:
    def __init__(self, nseq, nx, ny, chains, sites):
        self.nx, self.ny, self.nc = nx, ny, 2
        self.nz = nseq // (2 * ny)
        self.nd = self.ny * self.nz
        self.chains, self.sites = chains, sites
        self.rows = chains * sites
        self.hx = HEADS // nx
        self.total_sites = sites * nx
        self.half = self.total_sites // 2
        self.yrows = self.half // ny
        self.zrows = self.yrows // self.nz
        self.zpad = -(-(self.hx * self.zrows) // 16) * 16
        self.csites = sites // 2
        self.pair = 2 * chains
        self.cols = self.csites // self.nd
        self.drows = self.cols * self.pair
        self.col_len = self.nd * self.pair
        self.total_seqs = nseq * chains


def normed(wide, gain):
    center = wide - jnp.mean(wide, axis=-1, keepdims=True)
    spread = jnp.mean(center * center, axis=-1, keepdims=True)
    return (center * lax.rsqrt(spread + 1e-05) * gain).astype(BF)


def softmax(scores):
    top = jnp.max(scores, axis=-1, keepdims=True)
    e = jnp.exp(scores - top)
    return (e / jnp.sum(e, axis=-1, keepdims=True)).astype(BF)


def layer(
    D,
    a_ref, g1_ref, g2_ref,
    wq, wk, wv, wo, cq, ck, cv, co,
    out_ref,
    w_buf, xn, qkv_s, qkv_r, l_own, l_send, l_recv, y_send, y_recv, z_sum, z_send, z_recv,
    p_send, p_z, p_full, o_send, m_recv, a_res, mix, c_f32, c_send, c_recv, cn, c_qkv, c_mix,
    r_send, r_recv, f_send,
    w_sem, x_ss, x_rs, x_ls, a_sem, c_ss, c_rs, y_ss, y_rs, z_ss, z_rs, pz_ss, pz_rs, py_ss, py_rs,
    pc_sem, o_ss, o_rs, o_ls, i_ss, i_rs, i_ls, b_ss, b_rs, b_ls, f_sem,
):
    nx, ny, nz, nd, hx = D.nx, D.ny, D.nz, D.nd, D.hx
    seq, x = lax.axis_index("seq"), lax.axis_index("res")
    c = lax.rem(seq, 2)
    d = seq // 2
    y = lax.rem(d, ny)
    z = d // ny
    other = 1 - c

    def dev(z_, y_, c_, x_):
        return ((z_ * ny + y_) * 2 + c_, x_)

    sibling = dev(z, y, other, x)

    def remote(src, dst, ss, rs, to):
        return pltpu.make_async_remote_copy(
            src_ref=src, dst_ref=dst, send_sem=ss, recv_sem=rs, device_id=to, device_id_type=MESH
        )

    def loop(lo, hi, body):
        def step(k, carry):
            body(k)
            return carry

        lax.fori_loop(lo, hi, step, 0)

    def drain(ref, *sems):
        for sem in sems:
            pltpu.make_async_copy(ref, ref, sem).wait()

    weights = (wq, wk, wv, wo, cq, ck, cv, co)
    w_copies = [pltpu.make_async_copy(w, w_buf.at[n], w_sem.at[n]) for n, w in enumerate(weights)]
    for copy in w_copies:
        copy.start()

    bar = pltpu.get_barrier_semaphore()

    def greet(to):
        pl.semaphore_signal(bar, inc=1, device_id=to, device_id_type=MESH)

    def x_core(k):
        g = lax.rem(x * 2 + c + k, 2 * nx)
        return g // 2, lax.rem(g, 2)

    def greet_d(k):
        p = lax.rem(d + k, nd)
        greet(dev(p // ny, lax.rem(p, ny), c, x))

    def greet_x(k):
        xo, co_ = x_core(k)
        greet(dev(z, y, co_, xo))

    loop(1, nd, greet_d)
    loop(1, 2 * nx, greet_x)

    def norm_rows(s):
        xn[pl.ds(pl.multiple_of(s * D.sites, D.sites), D.sites), :] = normed(
            a_ref[s].astype(F32), g1_ref[...]
        )

    loop(0, D.chains, norm_rows)
    pl.semaphore_wait(bar, nd - 1 + 2 * nx - 1)

    a_half = pl.ds(pl.multiple_of(c * D.csites, D.csites), D.csites)
    a_other = pl.ds(pl.multiple_of(other * D.csites, D.csites), D.csites)
    a_local = pltpu.make_async_copy(a_ref.at[:, a_half, :], a_res.at[c], a_sem.at[0])
    a_local.start()
    a_copy = remote(a_ref.at[:, a_other, :], a_res.at[c], a_sem.at[1], a_sem.at[2], sibling)
    a_copy.start()

    my_sites = pl.ds(pl.multiple_of(x * D.sites, D.sites), D.sites)

    def x_copy(m, k):
        xo = lax.rem(x + k, nx)
        return remote(
            qkv_s.at[m, pl.ds(xo * hx, hx)], qkv_r.at[m, :, my_sites, :], x_ss.at[m], x_rs.at[m], dev(z, y, c, xo)
        )

    def x_local(m):
        return pltpu.make_async_copy(
            qkv_s.at[m, pl.ds(x * hx, hx)], qkv_r.at[m, :, my_sites, :], x_ls.at[m]
        )

    for m in range(3):
        w_copies[m].wait()

        def project(cb, m=m):
            cols = pl.ds(pl.multiple_of(cb * 256, 256), 256)
            t = jnp.dot(xn[...], w_buf[m, :, cols], preferred_element_type=F32).astype(BF)
            for hh in range(4):
                qkv_s[m, cb * 4 + hh] = jnp.concatenate(
                    [
                        t[s * D.sites : (s + 1) * D.sites, hh * HEAD : (hh + 1) * HEAD]
                        for s in range(D.chains)
                    ],
                    axis=-1,
                )

        loop(0, WIDTH // 256, project)
        x_local(m).start()
        loop(1, nx, lambda k, m=m: x_copy(m, k).start())

    def x_wait(m):
        x_local(m).wait()
        drain(qkv_r.at[m, :, pl.ds(0, (nx - 1) * D.sites), :], x_ss.at[m], x_rs.at[m])

    x_wait(0)
    x_wait(1)

    scale = 1.0 / (math.sqrt(HEAD) * math.sqrt(D.total_seqs))
    own_half = pl.ds(pl.multiple_of(c * D.half, D.half), D.half)
    far_half = pl.ds(pl.multiple_of(other * D.half, D.half), D.half)

    def c_copy(h):
        return remote(l_send.at[h], l_recv.at[h], c_ss.at[h], c_rs.at[h], sibling)

    def logits(h):
        keys = qkv_r[1, h]
        far = lax.dot_general(qkv_r[0, h, far_half, :], keys, NT, preferred_element_type=F32)
        l_send[h] = (far * scale).astype(BF)
        c_copy(h).start()
        own = lax.dot_general(qkv_r[0, h, own_half, :], keys, NT, preferred_element_type=F32)
        l_own[h] = own * scale

    loop(0, hx, logits)

    def y_rows(i):
        return pl.ds(pl.multiple_of(i * D.yrows, D.yrows), D.yrows)

    def y_copy(h, k):
        yo = lax.rem(y + k, ny)
        return remote(
            y_send.at[h, y_rows(yo), :], y_recv.at[y, h], y_ss.at[h], y_rs.at[h], dev(z, yo, c, x)
        )

    def core_sum(h):
        c_copy(h).wait()
        total = l_own[h] + l_recv[h].astype(F32)
        l_own[h] = total
        y_send[h] = total.astype(BF)
        loop(1, ny, lambda k: y_copy(h, k).start())

    loop(0, hx, core_sum)

    def y_sum(h):
        drain(y_recv.at[pl.ds(0, ny - 1), h], y_ss.at[h], y_rs.at[h])
        z_sum[h] = l_own[h, y_rows(y), :]

        def add(k):
            z_sum[h] += y_recv[lax.rem(y + k, ny), h].astype(F32)

        loop(1, ny, add)

    loop(0, hx, y_sum)

    zr = hx * D.zrows

    def z_fill(i):
        rows = pl.ds(pl.multiple_of(i * D.zrows, D.zrows), D.zrows)
        part = [z_sum[h, rows, :] for h in range(hx)]
        if D.zpad > zr:
            part.append(jnp.zeros((D.zpad - zr, D.total_sites), F32))
        z_send[i] = jnp.concatenate(part, axis=0).astype(BF)

    loop(0, nz, z_fill)

    def z_copy(k):
        zo = lax.rem(z + k, nz)
        return remote(z_send.at[zo], z_recv.at[z], z_ss, z_rs, dev(zo, y, c, x))

    loop(1, nz, lambda k: z_copy(k).start())
    drain(z_recv.at[pl.ds(0, nz - 1)], z_ss, z_rs)

    def z_add(k, total):
        return total + z_recv[lax.rem(z + k, nz)].astype(F32)

    tied = lax.fori_loop(1, nz, z_add, z_send[z].astype(F32))
    p_send[...] = softmax(tied)

    def pz_copy(k):
        zo = lax.rem(z + k, nz)
        return remote(p_send, p_z.at[z], pz_ss, pz_rs, dev(zo, y, c, x))

    loop(1, nz, lambda k: pz_copy(k).start())
    p_z[z] = p_send[...]
    drain(p_z.at[pl.ds(0, nz - 1)], pz_ss, pz_rs)

    def p_fill(i):
        rows = pl.ds(pl.multiple_of(i * D.zrows, D.zrows), D.zrows)
        block = p_z[i].astype(F32)
        for h in range(hx):
            z_sum[h, rows, :] = block[h * D.zrows : (h + 1) * D.zrows]

    loop(0, nz, p_fill)
    py_rows = pl.ds(pl.multiple_of(c * D.half + y * D.yrows, D.yrows), D.yrows)
    p_full[:, py_rows, :] = z_sum[...].astype(BF)

    def py_copy(k):
        yo = lax.rem(y + k, ny)
        return remote(
            p_full.at[:, py_rows, :], p_full.at[:, py_rows, :], py_ss, py_rs, dev(z, yo, c, x)
        )

    loop(1, ny, lambda k: py_copy(k).start())
    drain(p_full.at[:, pl.ds(0, (ny - 1) * D.yrows), :], py_ss, py_rs)
    pc_copy = remote(
        p_full.at[:, own_half, :], p_full.at[:, own_half, :], pc_sem.at[0], pc_sem.at[1], sibling
    )
    pc_copy.start()
    x_wait(2)
    pc_copy.wait()

    def o_rows(xo, co_):
        return pl.ds(pl.multiple_of(xo * D.sites + co_ * D.csites, D.csites), D.csites)

    def o_copy(h, k):
        xo, co_ = x_core(k)
        return remote(
            o_send.at[h, o_rows(xo, co_), :], m_recv.at[c, x * hx + h], o_ss, o_rs, dev(z, y, co_, xo)
        )

    def attend(h):
        o_send[h] = jnp.dot(p_full[h], qkv_r[2, h], preferred_element_type=F32).astype(BF)
        loop(1, 2 * nx, lambda k: o_copy(h, k).start())

    loop(0, hx, attend)
    o_local = pltpu.make_async_copy(
        o_send.at[:, o_rows(x, c), :], m_recv.at[c, pl.ds(x * hx, hx)], o_ls
    )
    o_local.start()
    drain(o_send.at[:, pl.ds(0, (2 * nx - 1) * D.csites), :], o_ss, o_rs)
    o_local.wait()

    for n in range(3, 8):
        w_copies[n].wait()
    a_local.wait()
    a_copy.wait()

    half_rows = D.chains * D.csites
    for cc in range(2):
        for s in range(D.chains):
            mix[s * D.csites : (s + 1) * D.csites, :] = jnp.concatenate(
                [m_recv[cc, h, :, s * HEAD : (s + 1) * HEAD] for h in range(HEADS)], axis=-1
            )

        def mixing(cb, cc=cc):
            cols = pl.ds(pl.multiple_of(cb * 256, 256), 256)
            inc = jnp.dot(mix[...], w_buf[3, :, cols], preferred_element_type=F32)
            for s in range(D.chains):
                after = a_res[cc, s, :, cols].astype(F32) + inc[s * D.csites : (s + 1) * D.csites]
                for j in range(2):
                    c_f32[cb * 2 + j, pl.ds(cc * D.chains + s, D.csites, stride=D.pair), :] = after[
                        :, j * LANES : (j + 1) * LANES
                    ]

        loop(0, WIDTH // 256, mixing)

    def to_bf(dst):
        def part(i):
            rows = pl.ds(pl.multiple_of(i * 64, 64), 64)
            for j in range(SLABS):
                dst[rows, j * LANES : (j + 1) * LANES] = c_f32[j, rows, :].astype(BF)

        loop(0, D.rows // 64, part)

    def from_bf(src):
        def part(i):
            rows = pl.ds(pl.multiple_of(i * 64, 64), 64)
            for j in range(SLABS):
                c_f32[j, rows, :] = src[rows, j * LANES : (j + 1) * LANES].astype(F32)

        loop(0, D.rows // 64, part)

    def d_rows(i):
        return pl.ds(pl.multiple_of(i * D.drows, D.drows), D.drows)

    def exchange(src, dst, ss, rs, ls):
        def copy(k):
            p = lax.rem(d + k, nd)
            return remote(
                src.at[d_rows(p), :], dst.at[d_rows(d), :], ss, rs, dev(p // ny, lax.rem(p, ny), c, x)
            )

        keep = pltpu.make_async_copy(src.at[d_rows(d), :], dst.at[d_rows(d), :], ls)
        loop(1, nd, lambda k: copy(k).start())
        keep.start()
        drain(dst.at[pl.ds(0, (nd - 1) * D.drows), :], ss, rs)
        keep.wait()

    to_bf(c_send)
    exchange(c_send, c_recv, i_ss, i_rs, i_ls)
    from_bf(c_recv)

    col_scale = 1.0 / math.sqrt(HEAD)
    lane = lax.broadcasted_iota(jnp.int32, (1, 2 * HEAD), 1)

    def column(r):
        def rows_of(p):
            return pl.ds(pl.multiple_of(p * D.drows + r * D.pair, D.pair), D.pair)

        wide = jnp.concatenate(
            [
                jnp.concatenate([c_f32[j, rows_of(p), :] for p in range(nd)], axis=0)
                for j in range(SLABS)
            ],
            axis=1,
        )
        cn[...] = normed(wide, g2_ref[...])
        for m in range(3):
            c_qkv[m] = jnp.dot(cn[...], w_buf[4 + m], preferred_element_type=F32).astype(BF)

        def two_heads(p):
            cols = pl.ds(pl.multiple_of(p * 2 * HEAD, 2 * HEAD), 2 * HEAD)
            q, k, v = c_qkv[0, :, cols], c_qkv[1, :, cols], c_qkv[2, :, cols]
            mixed = None
            for side in range(2):
                mine = (lane < HEAD) if side == 0 else (lane >= HEAD)
                zero = jnp.zeros_like(k)
                scores = lax.dot_general(
                    q, jnp.where(mine, k, zero), NT, preferred_element_type=F32
                )
                prob = softmax(scores * col_scale)
                part = jnp.dot(prob, jnp.where(mine, v, zero), preferred_element_type=F32)
                mixed = part if mixed is None else mixed + part
            c_mix[:, cols] = mixed.astype(BF)

        loop(0, HEADS // 2, two_heads)
        change = jnp.dot(c_mix[...], w_buf[7], preferred_element_type=F32)
        for p in range(nd):
            rows = rows_of(p)
            for j in range(SLABS):
                c_f32[j, rows, :] += change[p * D.pair : (p + 1) * D.pair, j * LANES : (j + 1) * LANES]

    loop(0, D.cols, column)

    to_bf(r_send)
    exchange(r_send, r_recv, b_ss, b_rs, b_ls)
    from_bf(r_recv)

    def chain_rows(s):
        rows = pl.ds(s, D.csites, stride=D.pair)
        return jnp.concatenate([c_f32[j, rows, :] for j in range(SLABS)], axis=1).astype(BF)

    for s in range(D.chains):
        f_send[s] = chain_rows(other * D.chains + s)
    f_copy = remote(f_send, out_ref.at[:, a_half, :], f_sem.at[0], f_sem.at[1], sibling)
    f_copy.start()
    for s in range(D.chains):
        out_ref[s, a_half, :] = chain_rows(c * D.chains + s)
    f_copy.wait()


def on_device(D, a, g1, wq, wk, wv, wo, g2, cq, ck, cv, co):
    vmem = pl.BlockSpec(memory_space=pltpu.VMEM)
    hbm = pl.BlockSpec(memory_space=pl.ANY)
    sites = D.total_sites
    R = D.rows
    bf = lambda *shape: pltpu.VMEM(shape, BF)
    f32 = lambda *shape: pltpu.VMEM(shape, F32)
    sem = pltpu.SemaphoreType.DMA
    scratch = dict(
        w_buf=bf(8, WIDTH, WIDTH),
        xn=bf(R, WIDTH),
        qkv_s=bf(3, HEADS, D.sites, D.chains * HEAD),
        qkv_r=bf(3, D.hx, sites, D.chains * HEAD),
        l_own=f32(D.hx, D.half, sites),
        l_send=bf(D.hx, D.half, sites),
        l_recv=bf(D.hx, D.half, sites),
        y_send=bf(D.hx, D.half, sites),
        y_recv=bf(D.ny, D.hx, D.yrows, sites),
        z_sum=f32(D.hx, D.yrows, sites),
        z_send=bf(D.nz, D.zpad, sites),
        z_recv=bf(D.nz, D.zpad, sites),
        p_send=bf(D.zpad, sites),
        p_z=bf(D.nz, D.zpad, sites),
        p_full=bf(D.hx, sites, sites),
        o_send=bf(D.hx, sites, D.chains * HEAD),
        m_recv=bf(2, HEADS, D.csites, D.chains * HEAD),
        a_res=bf(2, D.chains, D.csites, WIDTH),
        mix=bf(D.chains * D.csites, WIDTH),
        c_f32=f32(SLABS, R, LANES),
        c_send=bf(R, WIDTH),
        c_recv=bf(R, WIDTH),
        cn=bf(D.col_len, WIDTH),
        c_qkv=bf(3, D.col_len, WIDTH),
        c_mix=bf(D.col_len, WIDTH),
        r_send=bf(R, WIDTH),
        r_recv=bf(R, WIDTH),
        f_send=bf(D.chains, D.csites, WIDTH),
        w_sem=sem((8,)),
        x_ss=sem((3,)), x_rs=sem((3,)), x_ls=sem((3,)), a_sem=sem((3,)),
        c_ss=sem((D.hx,)), c_rs=sem((D.hx,)), y_ss=sem((D.hx,)), y_rs=sem((D.hx,)),
        z_ss=sem, z_rs=sem, pz_ss=sem, pz_rs=sem, py_ss=sem, py_rs=sem, pc_sem=sem((2,)),
        o_ss=sem, o_rs=sem, o_ls=sem, i_ss=sem, i_rs=sem, i_ls=sem, b_ss=sem, b_rs=sem, b_ls=sem,
        f_sem=sem((2,)),
    )
    flops = 2 * (8 * R * WIDTH * WIDTH + 2 * D.hx * sites * sites * D.chains * HEAD)
    return pl.pallas_call(
        functools.partial(layer, D),
        out_shape=jax.ShapeDtypeStruct(a.shape, a.dtype),
        in_specs=[vmem] * 3 + [hbm] * 8,
        out_specs=vmem,
        scratch_shapes=list(scratch.values()),
        compiler_params=pltpu.CompilerParams(
            collective_id=0, has_side_effects=True, vmem_limit_bytes=60 * 2**20
        ),
        cost_estimate=pl.CostEstimate(flops=flops, bytes_accessed=12 * 2**20, transcendentals=2**21),
        name="msa_layer",
    )(a, g1.reshape(1, -1), g2.reshape(1, -1), wq, wk, wv, wo, cq, ck, cv, co)


def solution(mesh):
    nseq, nx = mesh.shape["seq"], mesh.shape["res"]
    ny = 4 if nseq >= 32 else 2

    def step(a, *rest):
        D = Dims(nseq, nx, ny, a.shape[0], a.shape[1])
        return on_device(D, a, *rest)

    in_specs = (P("seq", "res", None),) + (P(),) * 10
    return jax.shard_map(
        step, mesh=mesh, in_specs=in_specs, out_specs=P("seq", "res", None), check_vma=False
    )
```

time: 422 us -> 147 us (0.35)
  waiting for transfers between devices: 279 us -> 0 us
  Pallas kernels: 0 us -> 141 us
  blocking collectives: 62.9 us -> 0 us
  matrix products: 29.3 us -> 0 us
  local copies, waits for them, and re-layouts: 21 us -> 4.61 us
  other arithmetic: 15.8 us -> 0 us
  between operations: 13.4 us -> 0.01 us
    psum x1 -> x0, waiting for transfers between devices: 189 us -> none  [on_device(): tied = lax.psum(partial_logits, 'seq')]
    pallas_call x0 -> x1, Pallas kernels: none -> 141 us  [on_device(): pl.pallas_call(functools.partial(layer, D), out_shape=jax.ShapeDtypeStruc...]
    all_gather x2 -> x0, waiting for transfers between devices: 89.9 us -> none  [the longest x1 46.2 us: on_device(): lax.all_gather(row_k, 'res', axis=1, tiled=True)]
    all_to_all x2 -> x0, blocking collectives: 62.9 us -> none  [the longest x1 34.1 us: on_device(): lax.all_to_all(grouped, 'seq', split_axis=1, concat_axis=0, tiled=True)]
    dot_general x12 -> x0, matrix products: 29.3 us -> none  [the longest x6 9.87 us: project(): jnp.dot(standardized_hidden.reshape(-1, embedding_dimension), weight, pre...]
    reshape x11 -> x2, local copies, waits for them, and re-layouts: 13.9 us -> 2.54 us  [the longest x1 1.28 us: on_device(): g2.reshape(1, -1)]
    sub x2 -> x0, other arithmetic: 7.8 us -> none  [the longest x1 4.24 us: on_device(): col_prob = jax.nn.softmax(scores, axis=-1).astype(jnp.bfloat16)]
    reduce_sum x4 -> x0, other arithmetic: 5.38 us -> none  [the longest x2 3.13 us: standardize_activations(): spread = jnp.mean(center * center, axis=-1, keepdims=True)]
  transfers between devices with their start and end apart: 3 -> 0, of which waited for: 3 -> 0; matrix products, arithmetic and copies ran while one was open for 2% -> 0% of each run, Pallas kernels for 0% -> 0%
where the time goes in v1:
time: 147 us; the launch traced here: 146 us
  Pallas kernels  141 us (96%)
  local copies, waits for them, and re-layouts  4.61 us (3%)
    pallas_call x1, Pallas kernels, on_device(): pl.pallas_call(functools.partial(layer, D), out_shape=jax.ShapeDtypeStruc...  141 us

profile of v1, /device:TPU:1, one launch (start us, length us, event | category | flops | bytes accessed | tf_op | source)
XLA Modules:
  0.0 146.1 jit_solution(5096786073965958775)
XLA Ops:
  0.0 1.3 reshape.6.g1_ref
  1.3 1.3 reshape.7.g2_ref
  2.5 141.4 %msa_layer.1 = bf16[4,128,768]{2,1,0:T(8,128)(2,1)} custom-call(bf16[4,128,768]{2,1,0:T(8,128)(2,1)} %a_ref.1, f32[1,768]{1,0:T(1,128)} %reshape.6.g1_ref, f32[1,768]{1,0:T(1,128)} %reshape.7.g2_ref, bf16[768,768]{1,0:T(8,128)(2,1)} %wq.1, bf16[768,768]{1,0:T(8,128)(2,1)} %wk.1, bf16[768,768]{1,0:T(8,128)(2,1)} %wv.1, bf16[768,768]{1,0:T(8,128)(2,1)} %wo.1, ...), custom_call_target="tpu_custom_call" | custom-call | flops 5637144576 | bytes 12582912 | tf_op jit(solution)/shard_map/msa_layer/pallas_call | solution.py:462
  144.0 2.1 %copy.13 = bf16[4,128,768]{2,1,0:T(8,128)(2,1)} copy(bf16[4,128,768]{2,1,0:T(8,128)(2,1)} %msa_layer.1) | data formatting | bytes 1572864

commit v2 on v0

v2 whole, which is shorter than its diff:
```python
import functools
import math

import jax
import jax.numpy as jnp
from jax import lax
from jax.experimental import pallas as pl
from jax.experimental.pallas import tpu as pltpu
from jax.sharding import PartitionSpec as P

MESH = pl.DeviceIdType.MESH
HEADS = 12
HEAD = 64
WIDTH = HEADS * HEAD
LANES = 128
SLABS = WIDTH // LANES
BF = jnp.bfloat16
F32 = jnp.float32
NT = (((1,), (1,)), ((), ()))


class Dims:
    def __init__(self, nseq, nx, ny, chains, sites):
        self.nx, self.ny = nx, ny
        self.nz = nseq // (2 * ny)
        self.nd = self.ny * self.nz
        self.chains, self.sites = chains, sites
        self.rows = chains * sites
        self.hx = HEADS // nx
        self.total_sites = sites * nx
        self.parts = sites // (2 * self.nd)
        self.psites = sites // self.parts
        self.csites = self.psites // 2
        self.prows = self.psites * nx
        self.half = self.prows // 2
        self.yrows = self.half // ny
        self.zrows = self.yrows // self.nz
        self.zpad = -(-(self.hx * self.zrows) // 16) * 16
        self.pair = 2 * chains
        self.col_len = self.nd * self.pair
        self.total_seqs = nseq * chains
        assert self.csites == self.nd and self.pair == 8


def normed(wide, gain):
    center = wide - jnp.mean(wide, axis=-1, keepdims=True)
    spread = jnp.mean(center * center, axis=-1, keepdims=True)
    return (center * lax.rsqrt(spread + 1e-05) * gain).astype(BF)


def softmax(scores):
    top = jnp.max(scores, axis=-1, keepdims=True)
    e = jnp.exp(scores - top)
    return (e / jnp.sum(e, axis=-1, keepdims=True)).astype(BF)


def layer(
    D,
    a_ref, g1_ref, g2_ref,
    wq, wk, wv, wo, cq, ck, cv, co,
    out_ref,
    w_buf, xn, qkv_s, q_r, k_r, v_r, l_own, l_send, l_recv, y_send, y_recv, z_sum, z_send, z_recv,
    p_send, p_z, p_full, o_send, m_recv, a_res, mix, c_f32, c_send, c_recv, wide_buf, cn, c_qkv, c_mix,
    r_send, r_recv, f_send,
    w_sem, x_ss, x_rs, x_ls, a_ls, a_ss, a_rs, c_ss, c_rs, y_ss, y_rs, z_ss, z_rs, pz_ss, pz_rs, py_ss, py_rs,
    pc_ss, pc_rs, o_ss, o_rs, o_ls, i_ss, i_rs, i_ls, b_ss, b_rs, b_ls, f_ss, f_rs,
):
    nx, ny, nz, nd, hx = D.nx, D.ny, D.nz, D.nd, D.hx
    seq, x = lax.axis_index("seq"), lax.axis_index("res")
    c = lax.rem(seq, 2)
    d = seq // 2
    y = lax.rem(d, ny)
    z = d // ny
    other = 1 - c

    def dev(z_, y_, c_, x_):
        return ((z_ * ny + y_) * 2 + c_, x_)

    def dev_d(p):
        return dev(p // ny, lax.rem(p, ny), c, x)

    sibling = dev(z, y, other, x)

    def remote(src, dst, ss, rs, to):
        return pltpu.make_async_remote_copy(
            src_ref=src, dst_ref=dst, send_sem=ss, recv_sem=rs, device_id=to, device_id_type=MESH
        )

    def loop(lo, hi, body):
        def step(k, carry):
            body(k)
            return carry

        lax.fori_loop(lo, hi, step, 0)

    def drain(ref, *sems):
        for sem in sems:
            pltpu.make_async_copy(ref, ref, sem).wait()

    def block(i, n):
        return pl.ds(pl.multiple_of(i * n, n), n)

    weights = (wq, wk, wv, wo, cq, ck, cv, co)
    w_copies = [pltpu.make_async_copy(w, w_buf.at[n], w_sem.at[n]) for n, w in enumerate(weights)]
    for n in (1, 0, 2, 3, 4, 5, 6, 7):
        w_copies[n].start()

    bar = pltpu.get_barrier_semaphore()

    def greet(to):
        pl.semaphore_signal(bar, inc=1, device_id=to, device_id_type=MESH)

    def x_core(k):
        g = lax.rem(x * 2 + c + k, 2 * nx)
        return g // 2, lax.rem(g, 2)

    def greet_x(k):
        xo, co_ = x_core(k)
        greet(dev(z, y, co_, xo))

    loop(1, 2 * nx, greet_x)
    loop(1, nd, lambda k: greet(dev_d(lax.rem(d + k, nd))))

    def norm_rows(s):
        xn[block(s, D.sites), :] = normed(a_ref[s].astype(F32), g1_ref[...].reshape(1, WIDTH))

    loop(0, D.chains, norm_rows)

    def project(m):
        w_copies[m].wait()

        def columns(cb):
            cols = block(cb, 256)
            t = jnp.dot(xn[...], w_buf[m, :, cols], preferred_element_type=F32).astype(BF)
            for hh in range(4):
                qkv_s[m, cb * 4 + hh] = jnp.concatenate(
                    [
                        t[s * D.sites : (s + 1) * D.sites, hh * HEAD : (hh + 1) * HEAD]
                        for s in range(D.chains)
                    ],
                    axis=-1,
                )

        loop(0, WIDTH // 256, columns)

    my_sites = block(x, D.sites)
    my_part = block(x, D.psites)

    def kv_copies(m, dst, n):
        def copy(k):
            xo = lax.rem(x + k, nx)
            return remote(
                qkv_s.at[m, block(xo, hx)], dst.at[:, my_sites, :], x_ss.at[n], x_rs.at[n], dev(z, y, c, xo)
            )

        keep = pltpu.make_async_copy(qkv_s.at[m, block(x, hx)], dst.at[:, my_sites, :], x_ls.at[n])
        return copy, keep

    def q_copies(r):
        rows = pl.ds(r * D.psites, D.psites)

        def copy(k):
            xo = lax.rem(x + k, nx)
            return remote(
                qkv_s.at[0, block(xo, hx), rows, :],
                q_r.at[r, :, my_part, :],
                x_ss.at[2 + r],
                x_rs.at[2 + r],
                dev(z, y, c, xo),
            )

        keep = pltpu.make_async_copy(
            qkv_s.at[0, block(x, hx), rows, :], q_r.at[r, :, my_part, :], x_ls.at[2 + r]
        )
        return copy, keep

    def x_start(copies):
        copy, keep = copies
        loop(1, nx, lambda k: copy(k).start())
        keep.start()

    def x_wait(copies, ref, n):
        copies[1].wait()
        drain(ref, x_ss.at[n], x_rs.at[n])

    k_copies, v_copies = kv_copies(1, k_r, 0), kv_copies(2, v_r, 1)
    kv_size = pl.ds(0, (nx - 1) * D.sites)
    q_size = pl.ds(0, (nx - 1) * D.psites)

    project(1)
    pl.semaphore_wait(bar, nd - 1 + 2 * nx - 1)
    x_start(k_copies)
    project(0)
    for r in range(D.parts):
        x_start(q_copies(r))

    def a_rows(r, core):
        return block(r * 2 + core, D.csites)

    a_copies = []
    for r in range(D.parts):
        keep = pltpu.make_async_copy(a_ref.at[:, a_rows(r, c), :], a_res.at[r, c], a_ls.at[r])
        swap = remote(a_ref.at[:, a_rows(r, other), :], a_res.at[r, c], a_ss.at[r], a_rs.at[r], sibling)
        keep.start()
        swap.start()
        a_copies.append((keep, swap))

    project(2)

    scale = 1.0 / (math.sqrt(HEAD) * math.sqrt(D.total_seqs))
    own_half, far_half = block(c, D.half), block(other, D.half)

    def c_copy(r, h):
        return remote(l_send.at[r, h], l_recv.at[r, h], c_ss.at[r, h], c_rs.at[r, h], sibling)

    def logits(r):
        def far_part(h):
            far = lax.dot_general(q_r[r, h, far_half, :], k_r[h], NT, preferred_element_type=F32)
            l_send[r, h] = (far * scale).astype(BF)
            c_copy(r, h).start()

        def own_part(h):
            own = lax.dot_general(q_r[r, h, own_half, :], k_r[h], NT, preferred_element_type=F32)
            l_own[r, h] = own * scale

        loop(0, hx, far_part)
        loop(0, hx, own_part)

    def y_copy(r, k):
        yo = lax.rem(y + k, ny)
        return remote(
            y_send.at[r, :, block(yo, D.yrows), :], y_recv.at[r, y], y_ss.at[r], y_rs.at[r], dev(z, yo, c, x)
        )

    def core_sum(r):
        def one(h):
            c_copy(r, h).wait()
            total = l_own[r, h] + l_recv[r, h].astype(F32)
            l_own[r, h] = total
            y_send[r, h] = total.astype(BF)

        loop(0, hx, one)
        loop(1, ny, lambda k: y_copy(r, k).start())

    def z_copy(r, k):
        zo = lax.rem(z + k, nz)
        return remote(z_send.at[r, zo], z_recv.at[r, z], z_ss.at[r], z_rs.at[r], dev(zo, y, c, x))

    def y_sum(r):
        drain(y_recv.at[r, pl.ds(0, ny - 1)], y_ss.at[r], y_rs.at[r])
        for h in range(hx):
            total = l_own[r, h, block(y, D.yrows), :]
            for k in range(1, ny):
                total += y_recv[r, lax.rem(y + k, ny), h].astype(F32)
            z_sum[h] = total
        spare = D.zpad - hx * D.zrows
        for i in range(nz):
            part = [z_sum[h, i * D.zrows : (i + 1) * D.zrows, :] for h in range(hx)]
            if spare:
                part.append(jnp.zeros((spare, D.total_sites), F32))
            z_send[r, i] = jnp.concatenate(part, axis=0).astype(BF)
        loop(1, nz, lambda k: z_copy(r, k).start())

    def pz_copy(r, k):
        zo = lax.rem(z + k, nz)
        return remote(p_send.at[r], p_z.at[r, z], pz_ss.at[r], pz_rs.at[r], dev(zo, y, c, x))

    def z_softmax(r):
        drain(z_recv.at[r, pl.ds(0, nz - 1)], z_ss.at[r], z_rs.at[r])
        tied = z_send[r, z].astype(F32)
        for k in range(1, nz):
            tied += z_recv[r, lax.rem(z + k, nz)].astype(F32)
        prob = softmax(tied)
        p_send[r] = prob
        loop(1, nz, lambda k: pz_copy(r, k).start())
        p_z[r, z] = prob

    py_rows = block(c * ny + y, D.yrows)

    def py_copy(r, k):
        yo = lax.rem(y + k, ny)
        place = p_full.at[r, :, py_rows, :]
        return remote(place, place, py_ss.at[r], py_rs.at[r], dev(z, yo, c, x))

    def gather_z(r):
        drain(p_z.at[r, pl.ds(0, nz - 1)], pz_ss.at[r], pz_rs.at[r])
        for i in range(nz):
            wide = p_z[r, i].astype(F32)
            for h in range(hx):
                z_sum[h, i * D.zrows : (i + 1) * D.zrows, :] = wide[h * D.zrows : (h + 1) * D.zrows]
        p_full[r, :, py_rows, :] = z_sum[...].astype(BF)
        loop(1, ny, lambda k: py_copy(r, k).start())

    def pc_copy(r):
        place = p_full.at[r, :, own_half, :]
        return remote(place, place, pc_ss.at[r], pc_rs.at[r], sibling)

    def gather_y(r):
        drain(p_full.at[r, :, pl.ds(0, (ny - 1) * D.yrows), :], py_ss.at[r], py_rs.at[r])
        pc_copy(r).start()

    def o_rows(xo, core):
        return block(xo * 2 + core, D.csites)

    def o_copy(r, k):
        xo, co_ = x_core(k)
        return remote(
            o_send.at[r, :, o_rows(xo, co_), :],
            m_recv.at[r, c, block(x, hx)],
            o_ss.at[r],
            o_rs.at[r],
            dev(z, y, co_, xo),
        )

    def o_local(r):
        return pltpu.make_async_copy(
            o_send.at[r, :, o_rows(x, c), :], m_recv.at[r, c, block(x, hx)], o_ls.at[r]
        )

    def attend(r):
        pc_copy(r).wait()

        def one(h):
            o_send[r, h] = jnp.dot(p_full[r, h], v_r[h], preferred_element_type=F32).astype(BF)

        loop(0, hx, one)
        loop(1, 2 * nx, lambda k: o_copy(r, k).start())
        o_local(r).start()

    def pack(slabs):
        pieces = [v.reshape(nd, D.pair, LANES) for v in slabs]
        left = jnp.concatenate(pieces[: SLABS // 2], axis=-1)
        right = jnp.concatenate(pieces[SLABS // 2 :], axis=-1)
        return jnp.concatenate([left, right], axis=1).astype(BF).reshape(2 * D.col_len, WIDTH // 2)

    def unpack(packed):
        t = packed.reshape(nd, 2 * D.pair, WIDTH // 2).astype(F32)
        both = jnp.concatenate([t[:, : D.pair], t[:, D.pair :]], axis=-1)
        return both.reshape(D.col_len, WIDTH)

    def d_copies(r, src, dst, ss, rs, ls):
        def copy(k):
            p = lax.rem(d + k, nd)
            return remote(
                src.at[r, block(p, 2 * D.pair), :], dst.at[r, block(d, 2 * D.pair), :], ss.at[r], rs.at[r], dev_d(p)
            )

        mine = block(d, 2 * D.pair)
        keep = pltpu.make_async_copy(src.at[r, mine, :], dst.at[r, mine, :], ls.at[r])
        return copy, keep

    def d_start(r, *refs):
        copy, keep = d_copies(r, *refs)
        loop(1, nd, lambda k: copy(k).start())
        keep.start()

    def d_wait(r, src, dst, ss, rs, ls):
        d_copies(r, src, dst, ss, rs, ls)[1].wait()
        drain(dst.at[r, pl.ds(0, (nd - 1) * 2 * D.pair), :], ss.at[r], rs.at[r])

    into = (c_send, c_recv, i_ss, i_rs, i_ls)
    back = (r_send, r_recv, b_ss, b_rs, b_ls)

    def after_row(r):
        o_local(r).wait()
        drain(o_send.at[r, :, pl.ds(0, (2 * nx - 1) * D.csites), :], o_ss.at[r], o_rs.at[r])
        for copy in a_copies[r]:
            copy.wait()
        for cc in range(2):
            for s in range(D.chains):
                n = cc * D.chains + s
                mix[n * D.csites : (n + 1) * D.csites, :] = jnp.concatenate(
                    [m_recv[r, cc, h, :, s * HEAD : (s + 1) * HEAD] for h in range(HEADS)], axis=-1
                )

        def mixing(cb):
            cols = block(cb, 256)
            inc = jnp.dot(mix[...], w_buf[3, :, cols], preferred_element_type=F32)
            for cc in range(2):
                for s in range(D.chains):
                    n = cc * D.chains + s
                    after = a_res[r, cc, s, :, cols].astype(F32) + inc[n * D.csites : (n + 1) * D.csites]
                    for j in range(2):
                        c_f32[cb * 2 + j, pl.ds(n, D.csites, stride=D.pair), :] = after[
                            :, j * LANES : (j + 1) * LANES
                        ]

        loop(0, WIDTH // 256, mixing)
        c_send[r] = pack([c_f32[j] for j in range(SLABS)])
        d_start(r, *into)

    col_scale = 1.0 / math.sqrt(HEAD)
    lane = lax.broadcasted_iota(jnp.int32, (1, 2 * HEAD), 1)

    def column(r):
        d_wait(r, *into)
        wide = unpack(c_recv[r])
        wide_buf[...] = wide
        cn[...] = normed(wide, g2_ref[...].reshape(1, WIDTH))
        for m in range(3):
            c_qkv[m] = jnp.dot(cn[...], w_buf[4 + m], preferred_element_type=F32).astype(BF)

        def two_heads(p):
            cols = block(p, 2 * HEAD)
            q, k, v = c_qkv[0, :, cols], c_qkv[1, :, cols], c_qkv[2, :, cols]
            zero = jnp.zeros_like(k)
            mixed = None
            for side in range(2):
                mine = (lane < HEAD) if side == 0 else (lane >= HEAD)
                scores = lax.dot_general(
                    q, jnp.where(mine, k, zero), NT, preferred_element_type=F32
                )
                prob = softmax(scores * col_scale)
                part = jnp.dot(prob, jnp.where(mine, v, zero), preferred_element_type=F32)
                mixed = part if mixed is None else mixed + part
            c_mix[:, cols] = mixed.astype(BF)

        loop(0, HEADS // 2, two_heads)
        change = jnp.dot(c_mix[...], w_buf[7], preferred_element_type=F32)
        total = wide_buf[...] + change
        r_send[r] = pack([total[:, j * LANES : (j + 1) * LANES] for j in range(SLABS)])
        d_start(r, *back)

    def f_copy(r):
        return remote(f_send.at[r], out_ref.at[:, a_rows(r, c), :], f_ss.at[r], f_rs.at[r], sibling)

    def finish(r):
        d_wait(r, *back)
        total = unpack(r_recv[r])
        for j in range(SLABS):
            c_f32[j] = total[:, j * LANES : (j + 1) * LANES]

        def chain_rows(s):
            rows = pl.ds(s, D.csites, stride=D.pair)
            return jnp.concatenate([c_f32[j, rows, :] for j in range(SLABS)], axis=1).astype(BF)

        for s in range(D.chains):
            f_send[r, s] = chain_rows(other * D.chains + s)
        f_copy(r).start()
        for s in range(D.chains):
            out_ref[s, a_rows(r, c), :] = chain_rows(c * D.chains + s)

    q_sized = q_r.at[0, :, q_size, :]

    def first(r):
        x_wait(q_copies(r), q_sized, 2 + r)
        logits(r)

    x_wait(k_copies, k_r.at[:, kv_size, :], 0)
    first(0)
    x_start(v_copies)
    core_sum(0)
    first(1)
    y_sum(0)
    core_sum(1)
    z_softmax(0)
    y_sum(1)
    gather_z(0)
    z_softmax(1)
    gather_y(0)
    gather_z(1)
    x_wait(v_copies, v_r.at[:, kv_size, :], 1)
    attend(0)
    for n in range(3, 8):
        w_copies[n].wait()
    gather_y(1)
    after_row(0)
    attend(1)
    after_row(1)
    column(0)
    column(1)
    finish(0)
    finish(1)
    f_copy(0).wait()
    f_copy(1).wait()


def on_device(D, a, g1, wq, wk, wv, wo, g2, cq, ck, cv, co):
    vmem = pl.BlockSpec(memory_space=pltpu.VMEM)
    hbm = pl.BlockSpec(memory_space=pl.ANY)
    sites, N, L = D.total_sites, D.parts, D.chains * HEAD
    bf = lambda *shape: pltpu.VMEM(shape, BF)
    f32 = lambda *shape: pltpu.VMEM(shape, F32)
    sem = lambda *shape: pltpu.SemaphoreType.DMA(shape)
    scratch = dict(
        w_buf=bf(8, WIDTH, WIDTH),
        xn=bf(D.rows, WIDTH),
        qkv_s=bf(3, HEADS, D.sites, L),
        q_r=bf(N, D.hx, D.prows, L),
        k_r=bf(D.hx, sites, L),
        v_r=bf(D.hx, sites, L),
        l_own=f32(N, D.hx, D.half, sites),
        l_send=bf(N, D.hx, D.half, sites),
        l_recv=bf(N, D.hx, D.half, sites),
        y_send=bf(N, D.hx, D.half, sites),
        y_recv=bf(N, D.ny, D.hx, D.yrows, sites),
        z_sum=f32(D.hx, D.yrows, sites),
        z_send=bf(N, D.nz, D.zpad, sites),
        z_recv=bf(N, D.nz, D.zpad, sites),
        p_send=bf(N, D.zpad, sites),
        p_z=bf(N, D.nz, D.zpad, sites),
        p_full=bf(N, D.hx, D.prows, sites),
        o_send=bf(N, D.hx, D.prows, L),
        m_recv=bf(N, 2, HEADS, D.csites, L),
        a_res=bf(N, 2, D.chains, D.csites, WIDTH),
        mix=bf(D.pair * D.csites, WIDTH),
        c_f32=f32(SLABS, D.col_len, LANES),
        c_send=bf(N, 2 * D.col_len, WIDTH // 2),
        c_recv=bf(N, 2 * D.col_len, WIDTH // 2),
        wide_buf=f32(D.col_len, WIDTH),
        cn=bf(D.col_len, WIDTH),
        c_qkv=bf(3, D.col_len, WIDTH),
        c_mix=bf(D.col_len, WIDTH),
        r_send=bf(N, 2 * D.col_len, WIDTH // 2),
        r_recv=bf(N, 2 * D.col_len, WIDTH // 2),
        f_send=bf(N, D.chains, D.csites, WIDTH),
        w_sem=sem(8),
        x_ss=sem(2 + N), x_rs=sem(2 + N), x_ls=sem(2 + N),
        a_ls=sem(N), a_ss=sem(N), a_rs=sem(N),
        c_ss=sem(N, D.hx), c_rs=sem(N, D.hx),
        y_ss=sem(N), y_rs=sem(N), z_ss=sem(N), z_rs=sem(N),
        pz_ss=sem(N), pz_rs=sem(N), py_ss=sem(N), py_rs=sem(N), pc_ss=sem(N), pc_rs=sem(N),
        o_ss=sem(N), o_rs=sem(N), o_ls=sem(N),
        i_ss=sem(N), i_rs=sem(N), i_ls=sem(N), b_ss=sem(N), b_rs=sem(N), b_ls=sem(N),
        f_ss=sem(N), f_rs=sem(N),
    )
    flops = 2 * (8 * D.rows * WIDTH * WIDTH + 2 * D.hx * sites * sites * L)
    return pl.pallas_call(
        functools.partial(layer, D),
        out_shape=jax.ShapeDtypeStruct(a.shape, a.dtype),
        in_specs=[vmem] * 3 + [hbm] * 8,
        out_specs=vmem,
        scratch_shapes=list(scratch.values()),
        compiler_params=pltpu.CompilerParams(
            collective_id=0, has_side_effects=True, vmem_limit_bytes=60 * 2**20
        ),
        cost_estimate=pl.CostEstimate(flops=flops, bytes_accessed=12 * 2**20, transcendentals=2**21),
        name="msa_layer",
    )(a, g1, g2, wq, wk, wv, wo, cq, ck, cv, co)


def solution(mesh):
    nseq, nx = mesh.shape["seq"], mesh.shape["res"]
    ny = 4

    def step(a, *rest):
        D = Dims(nseq, nx, ny, a.shape[0], a.shape[1])
        return on_device(D, a, *rest)

    in_specs = (P("seq", "res", None),) + (P(),) * 10
    return jax.shard_map(
        step, mesh=mesh, in_specs=in_specs, out_specs=P("seq", "res", None), check_vma=False
    )
```

time: 422 us -> 111 us (0.26)
  waiting for transfers between devices: 279 us -> 0 us
  Pallas kernels: 0 us -> 108 us
  blocking collectives: 62.9 us -> 0 us
  matrix products: 29.3 us -> 0 us
  local copies, waits for them, and re-layouts: 21 us -> 2.06 us
  other arithmetic: 15.8 us -> 0 us
  between operations: 13.4 us -> 0.01 us
    psum x1 -> x0, waiting for transfers between devices: 189 us -> none  [on_device(): tied = lax.psum(partial_logits, 'seq')]
    pallas_call x0 -> x1, Pallas kernels: none -> 108 us  [on_device(): pl.pallas_call(functools.partial(layer, D), out_shape=jax.ShapeDtypeStruc...]
    all_gather x2 -> x0, waiting for transfers between devices: 89.9 us -> none  [the longest x1 46.2 us: on_device(): lax.all_gather(row_k, 'res', axis=1, tiled=True)]
    all_to_all x2 -> x0, blocking collectives: 62.9 us -> none  [the longest x1 34.1 us: on_device(): lax.all_to_all(grouped, 'seq', split_axis=1, concat_axis=0, tiled=True)]
    dot_general x12 -> x0, matrix products: 29.3 us -> none  [the longest x6 9.87 us: project(): jnp.dot(standardized_hidden.reshape(-1, embedding_dimension), weight, pre...]
    reshape x11 -> x0, local copies, waits for them, and re-layouts: 13.9 us -> none  [the longest x1 3.77 us: on_device(): project(col_normed, vertical_lookup_matrix)]
    sub x2 -> x0, other arithmetic: 7.8 us -> none  [the longest x1 4.24 us: on_device(): col_prob = jax.nn.softmax(scores, axis=-1).astype(jnp.bfloat16)]
    reduce_sum x4 -> x0, other arithmetic: 5.38 us -> none  [the longest x2 3.13 us: standardize_activations(): spread = jnp.mean(center * center, axis=-1, keepdims=True)]
  transfers between devices with their start and end apart: 3 -> 0, of which waited for: 3 -> 0; matrix products, arithmetic and copies ran while one was open for 2% -> 0% of each run, Pallas kernels for 0% -> 0%
where the time goes in v2:
time: 111 us; the launch traced here: 110 us
  Pallas kernels  108 us (97%)
  local copies, waits for them, and re-layouts  2.06 us (2%)
    pallas_call x1, Pallas kernels, on_device(): pl.pallas_call(functools.partial(layer, D), out_shape=jax.ShapeDtypeStruc...  108 us

profile of v2, /device:TPU:1, one launch (start us, length us, event | category | flops | bytes accessed | tf_op | source)
XLA Modules:
  0.0 110.3 jit_solution(3194978169218165196)
XLA Ops:
  0.0 108.3 %msa_layer.1 = bf16[4,128,768]{2,1,0:T(8,128)(2,1)} custom-call(bf16[4,128,768]{2,1,0:T(8,128)(2,1)} %a_ref.1, f32[768]{0:T(1024)} %g1_ref.1, f32[768]{0:T(1024)} %g2_ref.1, bf16[768,768]{1,0:T(8,128)(2,1)} %wq.1, bf16[768,768]{1,0:T(8,128)(2,1)} %wk.1, bf16[768,768]{1,0:T(8,128)(2,1)} %wv.1, bf16[768,768]{1,0:T(8,128)(2,1)} %wo.1, bf16[768,768]{1,0:T(8,128)(2,1)} %cq.1, ...), custom_call_target="tpu_custom_call" | custom-call | flops 5637144576 | bytes 12582912 | tf_op jit(solution)/shard_map/msa_layer/pallas_call | solution.py:528
  108.3 2.1 %copy.13 = bf16[4,128,768]{2,1,0:T(8,128)(2,1)} copy(bf16[4,128,768]{2,1,0:T(8,128)(2,1)} %msa_layer.1) | data formatting | bytes 1572864

commit v3 on v2

v3 whole, which is shorter than its diff:
```python
import functools
import math

import jax
import jax.numpy as jnp
from jax import lax
from jax.experimental import pallas as pl
from jax.experimental.pallas import tpu as pltpu
from jax.sharding import PartitionSpec as P

MESH = pl.DeviceIdType.MESH
HEADS = 12
HEAD = 64
WIDTH = HEADS * HEAD
LANES = 128
SLABS = WIDTH // LANES
BF = jnp.bfloat16
F32 = jnp.float32
NT = (((1,), (1,)), ((), ()))


class Dims:
    def __init__(self, nseq, nx, ny, chains, sites):
        self.nx, self.ny = nx, ny
        self.nz = nseq // (2 * ny)
        self.nd = self.ny * self.nz
        self.chains, self.sites = chains, sites
        self.rows = chains * sites
        self.hx = HEADS // nx
        self.total_sites = sites * nx
        self.parts = sites // (2 * self.nd)
        self.psites = sites // self.parts
        self.csites = self.psites // 2
        self.prows = self.psites * nx
        self.half = self.prows // 2
        self.yrows = self.half // ny
        self.zrows = self.yrows // self.nz
        self.pair = 2 * chains
        self.col_len = self.nd * self.pair
        self.total_seqs = nseq * chains
        assert self.csites == self.nd and self.pair == 8 and self.zrows == 4


def normed(wide, gain):
    center = wide - jnp.mean(wide, axis=-1, keepdims=True)
    spread = jnp.mean(center * center, axis=-1, keepdims=True)
    return (center * lax.rsqrt(spread + 1e-05) * gain).astype(BF)


def softmax(scores):
    top = jnp.max(scores, axis=-1, keepdims=True)
    e = jnp.exp(scores - top)
    return e / jnp.sum(e, axis=-1, keepdims=True)


def layer(
    D,
    a_ref, g1_ref, g2_ref,
    wq, wk, wv, wo, cq, ck, cv, co,
    out_ref,
    w_buf, xn, qkv_s, kv_r, q_r, l_own, l_send, l_recv, y_send, y_recv, z_send, z_recv,
    p_send, p_z, p_full, o_send, m_recv, a_res, mix, c_f32, c_send, c_recv, wide_buf, cn, c_qkv, c_mix,
    r_send, r_recv, f_send,
    w_sem, x_ss, x_rs, x_ls, a_ls, a_ss, a_rs, c_ss, c_rs, y_ss, y_rs, z_ss, z_rs, pz_ss, pz_rs, py_ss, py_rs,
    pc_ss, pc_rs, o_ss, o_rs, o_ls, i_ss, i_rs, i_ls, b_ss, b_rs, b_ls, f_ss, f_rs,
):
    nx, ny, nz, nd, hx = D.nx, D.ny, D.nz, D.nd, D.hx
    seq, x = lax.axis_index("seq"), lax.axis_index("res")
    c = lax.rem(seq, 2)
    d = seq // 2
    y = lax.rem(d, ny)
    z = d // ny
    other = 1 - c

    def dev(z_, y_, c_, x_):
        return ((z_ * ny + y_) * 2 + c_, x_)

    def dev_d(p):
        return dev(p // ny, lax.rem(p, ny), c, x)

    sibling = dev(z, y, other, x)

    def remote(src, dst, ss, rs, to):
        return pltpu.make_async_remote_copy(
            src_ref=src, dst_ref=dst, send_sem=ss, recv_sem=rs, device_id=to, device_id_type=MESH
        )

    def loop(lo, hi, body):
        def step(k, carry):
            body(k)
            return carry

        lax.fori_loop(lo, hi, step, 0)

    def drain(ref, *sems):
        for sem in sems:
            pltpu.make_async_copy(ref, ref, sem).wait()

    def block(i, n):
        return pl.ds(pl.multiple_of(i * n, n), n)

    weights = (wk, wv, wq, wo, cq, ck, cv, co)
    w_copies = [pltpu.make_async_copy(w, w_buf.at[n], w_sem.at[n]) for n, w in enumerate(weights)]
    for n in (0, 2):
        w_copies[n].start()

    bar = pltpu.get_barrier_semaphore()

    def greet(to):
        pl.semaphore_signal(bar, inc=1, device_id=to, device_id_type=MESH)

    def x_core(k):
        g = lax.rem(x * 2 + c + k, 2 * nx)
        return g // 2, lax.rem(g, 2)

    def greet_x(k):
        xo, co_ = x_core(k)
        greet(dev(z, y, co_, xo))

    loop(1, 2 * nx, greet_x)
    loop(1, nd, lambda k: greet(dev_d(lax.rem(d + k, nd))))

    def norm_rows(s):
        xn[block(s, D.sites), :] = normed(a_ref[s].astype(F32), g1_ref[...].reshape(1, WIDTH))

    loop(0, D.chains, norm_rows)

    def project(m, h):
        w = jnp.concatenate(
            [w_buf[m, :, (g * hx + h) * HEAD : (g * hx + h + 1) * HEAD] for g in range(nx)], axis=-1
        )
        t = jnp.dot(xn[...], w, preferred_element_type=F32).astype(BF)
        for g in range(nx):
            qkv_s[m, h, g] = jnp.concatenate(
                [
                    t[s * D.sites : (s + 1) * D.sites, g * HEAD : (g + 1) * HEAD]
                    for s in range(D.chains)
                ],
                axis=-1,
            )

    my_sites = block(x, D.sites)
    my_part = block(x, D.psites)

    class Cross:
        def __init__(self, m, h, r=None):
            self.sem = m * hx + h if r is None else (2 + r) * hx + h
            if r is None:
                self.dst = kv_r.at[m, h, my_sites, :]
                self.size = kv_r.at[m, h, pl.ds(0, (nx - 1) * D.sites), :]
                self.src = lambda g: qkv_s.at[m, h, g]
            else:
                self.dst = q_r.at[r, h, my_part, :]
                self.size = q_r.at[r, h, pl.ds(0, (nx - 1) * D.psites), :]
                self.src = lambda g: qkv_s.at[2, h, g, pl.ds(r * D.psites, D.psites), :]

        def copy(self, k):
            xo = lax.rem(x + k, nx)
            return remote(
                self.src(xo), self.dst, x_ss.at[self.sem], x_rs.at[self.sem], dev(z, y, c, xo)
            )

        def keep(self):
            return pltpu.make_async_copy(self.src(x), self.dst, x_ls.at[self.sem])

        def start(self):
            loop(1, nx, lambda k: self.copy(k).start())
            self.keep().start()

        def wait(self):
            self.keep().wait()
            drain(self.size, x_ss.at[self.sem], x_rs.at[self.sem])

    scale = 1.0 / (math.sqrt(HEAD) * math.sqrt(D.total_seqs))
    own_half, far_half = block(c, D.half), block(other, D.half)

    def c_copy(r, h):
        return remote(l_send.at[r, h], l_recv.at[r, h], c_ss.at[r, h], c_rs.at[r, h], sibling)

    def logits(r, h):
        if r == 0:
            Cross(0, h).wait()
        Cross(2, h, r).wait()
        far = lax.dot_general(q_r[r, h, far_half, :], kv_r[0, h], NT, preferred_element_type=F32)
        l_send[r, h] = (far * scale).astype(BF)
        c_copy(r, h).start()
        own = lax.dot_general(q_r[r, h, own_half, :], kv_r[0, h], NT, preferred_element_type=F32)
        l_own[r, h] = own * scale

    def y_copy(r, h, k):
        yo = lax.rem(y + k, ny)
        return remote(
            y_send.at[r, h, block(yo, D.yrows), :],
            y_recv.at[r, h, y],
            y_ss.at[r, h],
            y_rs.at[r, h],
            dev(z, yo, c, x),
        )

    def core_sum(r, h):
        c_copy(r, h).wait()
        total = l_own[r, h] + l_recv[r, h].astype(F32)
        l_own[r, h] = total
        y_send[r, h] = total.astype(BF)
        loop(1, ny, lambda k: y_copy(r, h, k).start())

    zr, slabs = D.zrows, D.total_sites // LANES
    zt = zr * slabs

    def fold(rows):
        n = rows.shape[0] // zr
        return jnp.concatenate(
            [
                rows[i * zr : (i + 1) * zr, j * LANES : (j + 1) * LANES]
                for i in range(n)
                for j in range(slabs)
            ],
            axis=0,
        )

    def unfold(tiles):
        n = tiles.shape[0] // zt
        return jnp.concatenate(
            [
                jnp.concatenate(
                    [tiles[i * zt + j * zr : i * zt + (j + 1) * zr] for i in range(n)], axis=0
                )
                for j in range(slabs)
            ],
            axis=1,
        )

    z_size = pl.ds(0, (nz - 1) * zt)

    def z_copy(r, h, k):
        zo = lax.rem(z + k, nz)
        return remote(
            z_send.at[r, h, block(zo, zt), :],
            z_recv.at[r, h, block(z, zt), :],
            z_ss.at[r, h],
            z_rs.at[r, h],
            dev(zo, y, c, x),
        )

    def y_sum(r, h):
        drain(y_recv.at[r, h, pl.ds(0, ny - 1)], y_ss.at[r, h], y_rs.at[r, h])
        total = l_own[r, h, block(y, D.yrows), :]
        for k in range(1, ny):
            total += y_recv[r, h, lax.rem(y + k, ny)].astype(F32)
        z_send[r, h] = fold(total).astype(BF)
        loop(1, nz, lambda k: z_copy(r, h, k).start())

    def pz_copy(r, h, k):
        zo = lax.rem(z + k, nz)
        return remote(
            p_send.at[r, h], p_z.at[r, h, block(z, zt), :], pz_ss.at[r, h], pz_rs.at[r, h], dev(zo, y, c, x)
        )

    def z_softmax(r, h):
        drain(z_recv.at[r, h, z_size, :], z_ss.at[r, h], z_rs.at[r, h])
        tied = z_send[r, h, block(z, zt), :].astype(F32)
        for k in range(1, nz):
            tied += z_recv[r, h, block(lax.rem(z + k, nz), zt), :].astype(F32)
        prob = fold(softmax(unfold(tied))).astype(BF)
        p_send[r, h] = prob
        loop(1, nz, lambda k: pz_copy(r, h, k).start())
        p_z[r, h, block(z, zt), :] = prob

    py_rows = block(c * ny + y, D.yrows)

    def py_copy(r, h, k):
        yo = lax.rem(y + k, ny)
        place = p_full.at[r, h, py_rows, :]
        return remote(place, place, py_ss.at[r, h], py_rs.at[r, h], dev(z, yo, c, x))

    def gather_z(r, h):
        drain(p_z.at[r, h, z_size, :], pz_ss.at[r, h], pz_rs.at[r, h])
        p_full[r, h, py_rows, :] = unfold(p_z[r, h].astype(F32)).astype(BF)
        loop(1, ny, lambda k: py_copy(r, h, k).start())

    def pc_copy(r, h):
        place = p_full.at[r, h, own_half, :]
        return remote(place, place, pc_ss.at[r, h], pc_rs.at[r, h], sibling)

    def gather_y(r, h):
        drain(p_full.at[r, h, pl.ds(0, (ny - 1) * D.yrows), :], py_ss.at[r, h], py_rs.at[r, h])
        pc_copy(r, h).start()

    def o_rows(xo, core):
        return block(xo * 2 + core, D.csites)

    def o_copy(r, h, k):
        xo, co_ = x_core(k)
        return remote(
            o_send.at[r, h, o_rows(xo, co_), :],
            m_recv.at[r, c, x * hx + h],
            o_ss.at[r, h],
            o_rs.at[r, h],
            dev(z, y, co_, xo),
        )

    def o_local(r, h):
        return pltpu.make_async_copy(
            o_send.at[r, h, o_rows(x, c), :], m_recv.at[r, c, x * hx + h], o_ls.at[r, h]
        )

    def attend(r, h):
        if r == 0:
            Cross(1, h).wait()
        pc_copy(r, h).wait()
        o_send[r, h] = jnp.dot(p_full[r, h], kv_r[1, h], preferred_element_type=F32).astype(BF)
        loop(1, 2 * nx, lambda k: o_copy(r, h, k).start())
        o_local(r, h).start()

    def pack(slabs):
        pieces = [v.reshape(nd, D.pair, LANES) for v in slabs]
        left = jnp.concatenate(pieces[: SLABS // 2], axis=-1)
        right = jnp.concatenate(pieces[SLABS // 2 :], axis=-1)
        return jnp.concatenate([left, right], axis=1).astype(BF).reshape(2 * D.col_len, WIDTH // 2)

    def unpack(packed):
        t = packed.reshape(nd, 2 * D.pair, WIDTH // 2).astype(F32)
        both = jnp.concatenate([t[:, : D.pair], t[:, D.pair :]], axis=-1)
        return both.reshape(D.col_len, WIDTH)

    def d_copies(r, src, dst, ss, rs, ls):
        def copy(k):
            p = lax.rem(d + k, nd)
            return remote(
                src.at[r, block(p, 2 * D.pair), :], dst.at[r, block(d, 2 * D.pair), :], ss.at[r], rs.at[r], dev_d(p)
            )

        mine = block(d, 2 * D.pair)
        keep = pltpu.make_async_copy(src.at[r, mine, :], dst.at[r, mine, :], ls.at[r])
        return copy, keep

    def d_start(r, *refs):
        copy, keep = d_copies(r, *refs)
        loop(1, nd, lambda k: copy(k).start())
        keep.start()

    def d_wait(r, src, dst, ss, rs, ls):
        d_copies(r, src, dst, ss, rs, ls)[1].wait()
        drain(dst.at[r, pl.ds(0, (nd - 1) * 2 * D.pair), :], ss.at[r], rs.at[r])

    into = (c_send, c_recv, i_ss, i_rs, i_ls)
    back = (r_send, r_recv, b_ss, b_rs, b_ls)

    def a_rows(r, core):
        return block(r * 2 + core, D.csites)

    def residual_copies():
        copies = []
        for r in range(D.parts):
            keep = pltpu.make_async_copy(a_ref.at[:, a_rows(r, c), :], a_res.at[r, c], a_ls.at[r])
            swap = remote(a_ref.at[:, a_rows(r, other), :], a_res.at[r, c], a_ss.at[r], a_rs.at[r], sibling)
            keep.start()
            swap.start()
            copies.append((keep, swap))
        return copies

    def after_row(r):
        for h in range(hx):
            o_local(r, h).wait()
            drain(o_send.at[r, h, pl.ds(0, (2 * nx - 1) * D.csites), :], o_ss.at[r, h], o_rs.at[r, h])
        for copy in a_copies[r]:
            copy.wait()
        for cc in range(2):
            for s in range(D.chains):
                n = cc * D.chains + s
                mix[n * D.csites : (n + 1) * D.csites, :] = jnp.concatenate(
                    [m_recv[r, cc, h, :, s * HEAD : (s + 1) * HEAD] for h in range(HEADS)], axis=-1
                )

        def mixing(cb):
            cols = block(cb, 256)
            inc = jnp.dot(mix[...], w_buf[3, :, cols], preferred_element_type=F32)
            for cc in range(2):
                for s in range(D.chains):
                    n = cc * D.chains + s
                    after = a_res[r, cc, s, :, cols].astype(F32) + inc[n * D.csites : (n + 1) * D.csites]
                    for j in range(2):
                        c_f32[cb * 2 + j, pl.ds(n, D.csites, stride=D.pair), :] = after[
                            :, j * LANES : (j + 1) * LANES
                        ]

        loop(0, WIDTH // 256, mixing)
        c_send[r] = pack([c_f32[j] for j in range(SLABS)])
        d_start(r, *into)

    col_scale = 1.0 / math.sqrt(HEAD)
    lane = lax.broadcasted_iota(jnp.int32, (1, 2 * HEAD), 1)

    def column(r):
        d_wait(r, *into)
        wide = unpack(c_recv[r])
        wide_buf[...] = wide
        cn[...] = normed(wide, g2_ref[...].reshape(1, WIDTH))
        for m in range(3):
            c_qkv[m] = jnp.dot(cn[...], w_buf[4 + m], preferred_element_type=F32).astype(BF)

        def two_heads(p):
            cols = block(p, 2 * HEAD)
            q, k, v = c_qkv[0, :, cols], c_qkv[1, :, cols], c_qkv[2, :, cols]
            zero = jnp.zeros_like(k)
            mixed = None
            for side in range(2):
                mine = (lane < HEAD) if side == 0 else (lane >= HEAD)
                scores = lax.dot_general(
                    q, jnp.where(mine, k, zero), NT, preferred_element_type=F32
                )
                prob = softmax(scores * col_scale).astype(BF)
                part = jnp.dot(prob, jnp.where(mine, v, zero), preferred_element_type=F32)
                mixed = part if mixed is None else mixed + part
            c_mix[:, cols] = mixed.astype(BF)

        loop(0, HEADS // 2, two_heads)
        change = jnp.dot(c_mix[...], w_buf[7], preferred_element_type=F32)
        total = wide_buf[...] + change
        r_send[r] = pack([total[:, j * LANES : (j + 1) * LANES] for j in range(SLABS)])
        d_start(r, *back)

    def f_copy(r):
        return remote(f_send.at[r], out_ref.at[:, a_rows(r, c), :], f_ss.at[r], f_rs.at[r], sibling)

    def finish(r):
        d_wait(r, *back)
        total = unpack(r_recv[r])
        for j in range(SLABS):
            c_f32[j] = total[:, j * LANES : (j + 1) * LANES]

        def chain_rows(s):
            rows = pl.ds(s, D.csites, stride=D.pair)
            return jnp.concatenate([c_f32[j, rows, :] for j in range(SLABS)], axis=1).astype(BF)

        for s in range(D.chains):
            f_send[r, s] = chain_rows(other * D.chains + s)
        f_copy(r).start()
        for s in range(D.chains):
            out_ref[s, a_rows(r, c), :] = chain_rows(c * D.chains + s)

    for m in (0, 2):
        w_copies[m].wait()
    for n in (1, 3, 4, 5, 6, 7):
        w_copies[n].start()

    def first(h):
        Cross(0, h).start()
        Cross(2, h, 0).start()

    project(0, 0)
    project(2, 0)
    pl.semaphore_wait(bar, nd - 1 + 2 * nx - 1)
    first(0)
    project(0, 1)
    project(2, 1)
    first(1)
    project(0, 2)
    project(2, 2)
    a_copies = residual_copies()
    w_copies[1].wait()
    for h in range(hx):
        project(1, h)

    def queries(h):
        Cross(2, h, 1).start()

    def values(h):
        Cross(1, h).start()

    def weights_in():
        for n in range(3, 8):
            w_copies[n].wait()

    plan = (
        (logits, 0, 0), (first, 2), (core_sum, 0, 0), (logits, 0, 1), (queries, 0), (queries, 1), (queries, 2),
        (core_sum, 0, 1), (y_sum, 0, 0), (logits, 0, 2), (values, 0), (values, 1), (values, 2),
        (core_sum, 0, 2), (y_sum, 0, 1), (z_softmax, 0, 0), (logits, 1, 0), (core_sum, 1, 0), (y_sum, 0, 2),
        (z_softmax, 0, 1), (gather_z, 0, 0), (logits, 1, 1), (core_sum, 1, 1), (y_sum, 1, 0), (z_softmax, 0, 2),
        (gather_z, 0, 1), (gather_y, 0, 0), (logits, 1, 2), (core_sum, 1, 2), (y_sum, 1, 1), (attend, 0, 0),
        (z_softmax, 1, 0), (gather_z, 0, 2), (gather_y, 0, 1), (y_sum, 1, 2), (attend, 0, 1), (z_softmax, 1, 1),
        (gather_z, 1, 0), (gather_y, 0, 2), (weights_in,), (attend, 0, 2), (z_softmax, 1, 2), (gather_z, 1, 1),
        (gather_y, 1, 0), (attend, 1, 0), (gather_z, 1, 2), (after_row, 0), (gather_y, 1, 1), (attend, 1, 1),
        (gather_y, 1, 2), (attend, 1, 2), (after_row, 1), (column, 0), (column, 1), (finish, 0), (finish, 1),
    )
    for step, *args in plan:
        step(*args)
    f_copy(0).wait()
    f_copy(1).wait()


def on_device(D, a, g1, wq, wk, wv, wo, g2, cq, ck, cv, co):
    vmem = pl.BlockSpec(memory_space=pltpu.VMEM)
    hbm = pl.BlockSpec(memory_space=pl.ANY)
    sites, N, H, L = D.total_sites, D.parts, D.hx, D.chains * HEAD
    bf = lambda *shape: pltpu.VMEM(shape, BF)
    f32 = lambda *shape: pltpu.VMEM(shape, F32)
    sem = lambda *shape: pltpu.SemaphoreType.DMA(shape)
    scratch = dict(
        w_buf=bf(8, WIDTH, WIDTH),
        xn=bf(D.rows, WIDTH),
        qkv_s=bf(3, D.hx, D.nx, D.sites, L),
        kv_r=bf(2, H, sites, L),
        q_r=bf(N, H, D.prows, L),
        l_own=f32(N, H, D.half, sites),
        l_send=bf(N, H, D.half, sites),
        l_recv=bf(N, H, D.half, sites),
        y_send=bf(N, H, D.half, sites),
        y_recv=bf(N, H, D.ny, D.yrows, sites),
        z_send=bf(N, H, D.yrows * sites // LANES, LANES),
        z_recv=bf(N, H, D.yrows * sites // LANES, LANES),
        p_send=bf(N, H, D.zrows * sites // LANES, LANES),
        p_z=bf(N, H, D.yrows * sites // LANES, LANES),
        p_full=bf(N, H, D.prows, sites),
        o_send=bf(N, H, D.prows, L),
        m_recv=bf(N, 2, HEADS, D.csites, L),
        a_res=bf(N, 2, D.chains, D.csites, WIDTH),
        mix=bf(D.pair * D.csites, WIDTH),
        c_f32=f32(SLABS, D.col_len, LANES),
        c_send=bf(N, 2 * D.col_len, WIDTH // 2),
        c_recv=bf(N, 2 * D.col_len, WIDTH // 2),
        wide_buf=f32(D.col_len, WIDTH),
        cn=bf(D.col_len, WIDTH),
        c_qkv=bf(3, D.col_len, WIDTH),
        c_mix=bf(D.col_len, WIDTH),
        r_send=bf(N, 2 * D.col_len, WIDTH // 2),
        r_recv=bf(N, 2 * D.col_len, WIDTH // 2),
        f_send=bf(N, D.chains, D.csites, WIDTH),
        w_sem=sem(8),
        x_ss=sem((2 + N) * H), x_rs=sem((2 + N) * H), x_ls=sem((2 + N) * H),
        a_ls=sem(N), a_ss=sem(N), a_rs=sem(N),
        c_ss=sem(N, H), c_rs=sem(N, H), y_ss=sem(N, H), y_rs=sem(N, H), z_ss=sem(N, H), z_rs=sem(N, H),
        pz_ss=sem(N, H), pz_rs=sem(N, H), py_ss=sem(N, H), py_rs=sem(N, H), pc_ss=sem(N, H), pc_rs=sem(N, H),
        o_ss=sem(N, H), o_rs=sem(N, H), o_ls=sem(N, H),
        i_ss=sem(N), i_rs=sem(N), i_ls=sem(N), b_ss=sem(N), b_rs=sem(N), b_ls=sem(N),
        f_ss=sem(N), f_rs=sem(N),
    )
    flops = 2 * (8 * D.rows * WIDTH * WIDTH + 2 * D.hx * sites * sites * L)
    return pl.pallas_call(
        functools.partial(layer, D),
        out_shape=jax.ShapeDtypeStruct(a.shape, a.dtype),
        in_specs=[vmem] * 3 + [hbm] * 8,
        out_specs=vmem,
        scratch_shapes=list(scratch.values()),
        compiler_params=pltpu.CompilerParams(
            collective_id=0, has_side_effects=True, vmem_limit_bytes=60 * 2**20
        ),
        cost_estimate=pl.CostEstimate(flops=flops, bytes_accessed=12 * 2**20, transcendentals=2**21),
        name="msa_layer",
    )(a, g1, g2, wq, wk, wv, wo, cq, ck, cv, co)


def solution(mesh):
    nseq, nx = mesh.shape["seq"], mesh.shape["res"]
    ny = 4

    def step(a, *rest):
        D = Dims(nseq, nx, ny, a.shape[0], a.shape[1])
        return on_device(D, a, *rest)

    in_specs = (P("seq", "res", None),) + (P(),) * 10
    return jax.shard_map(
        step, mesh=mesh, in_specs=in_specs, out_specs=P("seq", "res", None), check_vma=False
    )
```

time: 111 us -> 104 us (0.937)
  Pallas kernels: 108 us -> 102 us
    pallas_call x1, Pallas kernels: 108 us -> 102 us  [on_device(): pl.pallas_call(functools.partial(layer, D), out_shape=jax.ShapeDtypeStruc...]
where the time goes in v3:
time: 104 us
  Pallas kernels  102 us (98%)
  local copies, waits for them, and re-layouts  2.06 us (2%)
    pallas_call x1, Pallas kernels, on_device(): pl.pallas_call(functools.partial(layer, D), out_shape=jax.ShapeDtypeStruc...  102 us

profile of v3, /device:TPU:1, one launch (start us, length us, event | category | flops | bytes accessed | tf_op | source)
XLA Modules:
  0.0 104.3 jit_solution(11968171503860427691)
XLA Ops:
  0.0 102.2 %msa_layer.1 = bf16[4,128,768]{2,1,0:T(8,128)(2,1)} custom-call(bf16[4,128,768]{2,1,0:T(8,128)(2,1)} %a_ref.1, f32[768]{0:T(1024)} %g1_ref.1, f32[768]{0:T(1024)} %g2_ref.1, bf16[768,768]{1,0:T(8,128)(2,1)} %wq.1, bf16[768,768]{1,0:T(8,128)(2,1)} %wk.1, bf16[768,768]{1,0:T(8,128)(2,1)} %wv.1, bf16[768,768]{1,0:T(8,128)(2,1)} %wo.1, bf16[768,768]{1,0:T(8,128)(2,1)} %cq.1, ...), custom_call_target="tpu_custom_call" | custom-call | flops 5637144576 | bytes 12582912 | tf_op jit(solution)/shard_map/msa_layer/pallas_call | solution.py:539
  102.2 2.1 %copy.13 = bf16[4,128,768]{2,1,0:T(8,128)(2,1)} copy(bf16[4,128,768]{2,1,0:T(8,128)(2,1)} %msa_layer.1) | data formatting | bytes 1572864

commit v4 on v3

--- a/solution.py
+++ b/solution.py
@@ -99,6 +99,11 @@
     def block(i, n):
         return pl.ds(pl.multiple_of(i * n, n), n)
 
+    def turn(i, n):
+        j = n - 1 - i
+        far = (j + 1) // 2
+        return lax.rem(far + (n - 2 * far) * lax.rem(j + 1, 2), n)
+
     weights = (wk, wv, wq, wo, cq, ck, cv, co)
     w_copies = [pltpu.make_async_copy(w, w_buf.at[n], w_sem.at[n]) for n, w in enumerate(weights)]
     for n in (0, 2):
@@ -118,7 +123,8 @@
         greet(dev(z, y, co_, xo))
 
     loop(1, 2 * nx, greet_x)
-    loop(1, nd, lambda k: greet(dev_d(lax.rem(d + k, nd))))
+    loop(1, ny, lambda k: greet(dev(z, lax.rem(y + k, ny), c, x)))
+    loop(1, nz, lambda k: greet(dev(lax.rem(z + k, nz), y, c, x)))
 
     def norm_rows(s):
         xn[block(s, D.sites), :] = normed(a_ref[s].astype(F32), g1_ref[...].reshape(1, WIDTH))
@@ -233,7 +239,7 @@
     z_size = pl.ds(0, (nz - 1) * zt)
 
     def z_copy(r, h, k):
-        zo = lax.rem(z + k, nz)
+        zo = lax.rem(z + turn(k - 1, nz), nz)
         return remote(
             z_send.at[r, h, block(zo, zt), :],
             z_recv.at[r, h, block(z, zt), :],
@@ -251,7 +257,7 @@
         loop(1, nz, lambda k: z_copy(r, h, k).start())
 
     def pz_copy(r, h, k):
-        zo = lax.rem(z + k, nz)
+        zo = lax.rem(z + turn(k - 1, nz), nz)
         return remote(
             p_send.at[r, h], p_z.at[r, h, block(z, zt), :], pz_ss.at[r, h], pz_rs.at[r, h], dev(zo, y, c, x)
         )
@@ -325,7 +331,10 @@
 
     def d_copies(r, src, dst, ss, rs, ls):
         def copy(k):
-            p = lax.rem(d + k, nd)
+            j = nz - 1 - (k - 1) // ny
+            dz = turn((k - 1) // ny, nz)
+            dy = lax.rem(k - 1, ny) + jnp.where(j == 0, 1, 0)
+            p = lax.rem(z + dz, nz) * ny + lax.rem(y + dy, ny)
             return remote(
                 src.at[r, block(p, 2 * D.pair), :], dst.at[r, block(d, 2 * D.pair), :], ss.at[r], rs.at[r], dev_d(p)
             )
@@ -450,7 +459,7 @@
 
     project(0, 0)
     project(2, 0)
-    pl.semaphore_wait(bar, nd - 1 + 2 * nx - 1)
+    pl.semaphore_wait(bar, 2 * nx - 1 + ny - 1 + nz - 1)
     first(0)
     project(0, 1)
     project(2, 1)

time: 104 us -> 100 us (0.962)
  Pallas kernels: 102 us -> 98.2 us
    pallas_call x1, Pallas kernels: 102 us -> 98.2 us  [on_device(): pl.pallas_call(functools.partial(layer, D), out_shape=jax.ShapeDtypeStruc...]
where the time goes in v4:
time: 100 us
  Pallas kernels  98.2 us (98%)
  local copies, waits for them, and re-layouts  2.06 us (2%)
    pallas_call x1, Pallas kernels, on_device(): pl.pallas_call(functools.partial(layer, D), out_shape=jax.ShapeDtypeStruc...  98.2 us
    unnamed x1, local copies, waits for them, and re-layouts  2.06 us

profile of v4, /device:TPU:1, one launch (start us, length us, event | category | flops | bytes accessed | tf_op | source)
XLA Modules:
  0.0 100.3 jit_solution(12619833657864090590)
XLA Ops:
  0.0 98.2 %msa_layer.1 = bf16[4,128,768]{2,1,0:T(8,128)(2,1)} custom-call(bf16[4,128,768]{2,1,0:T(8,128)(2,1)} %a_ref.1, f32[768]{0:T(1024)} %g1_ref.1, f32[768]{0:T(1024)} %g2_ref.1, bf16[768,768]{1,0:T(8,128)(2,1)} %wq.1, bf16[768,768]{1,0:T(8,128)(2,1)} %wk.1, bf16[768,768]{1,0:T(8,128)(2,1)} %wv.1, bf16[768,768]{1,0:T(8,128)(2,1)} %wo.1, bf16[768,768]{1,0:T(8,128)(2,1)} %cq.1, ...), custom_call_target="tpu_custom_call" | custom-call | flops 5637144576 | bytes 12582912 | tf_op jit(solution)/shard_map/msa_layer/pallas_call | solution.py:548
  98.2 2.1 %copy.13 = bf16[4,128,768]{2,1,0:T(8,128)(2,1)} copy(bf16[4,128,768]{2,1,0:T(8,128)(2,1)} %msa_layer.1) | data formatting | bytes 1572864

commit v5 on v4

--- a/solution.py
+++ b/solution.py
@@ -55,14 +55,14 @@
 
 def layer(
     D,
-    a_ref, g1_ref, g2_ref,
+    a_hbm, g1_ref, g2_ref,
     wq, wk, wv, wo, cq, ck, cv, co,
     out_ref,
-    w_buf, xn, qkv_s, kv_r, q_r, l_own, l_send, l_recv, y_send, y_recv, z_send, z_recv,
-    p_send, p_z, p_full, o_send, m_recv, a_res, mix, c_f32, c_send, c_recv, wide_buf, cn, c_qkv, c_mix,
+    a_ref, out_v, w_buf, xn, qkv_s, kv_r, q_r, l_own, l_send, l_recv, y_send, y_recv, z_send, z_recv,
+    p_send, p_z, p_full, o_send, m_recv, wo_buf, acc, a_res, mix, c_f32, c_send, c_recv, wide_buf, cn, c_qkv, c_mix,
     r_send, r_recv, f_send,
-    w_sem, x_ss, x_rs, x_ls, a_ls, a_ss, a_rs, c_ss, c_rs, y_ss, y_rs, z_ss, z_rs, pz_ss, pz_rs, py_ss, py_rs,
-    pc_ss, pc_rs, o_ss, o_rs, o_ls, i_ss, i_rs, i_ls, b_ss, b_rs, b_ls, f_ss, f_rs,
+    w_sem, wo_sem, x_ss, x_rs, x_ls, a_ls, a_ss, a_rs, c_ss, c_rs, y_ss, y_rs, z_ss, z_rs, pz_ss, pz_rs, py_ss, py_rs,
+    pc_ss, pc_rs, o_ss, o_rs, o_ls, i_ss, i_rs, i_ls, b_ss, b_rs, b_ls, f_ss, f_rs, out_sem,
 ):
     nx, ny, nz, nd, hx = D.nx, D.ny, D.nz, D.nd, D.hx
     seq, x = lax.axis_index("seq"), lax.axis_index("res")
@@ -104,8 +104,11 @@
         far = (j + 1) // 2
         return lax.rem(far + (n - 2 * far) * lax.rem(j + 1, 2), n)
 
-    weights = (wk, wv, wq, wo, cq, ck, cv, co)
+    weights = (wk, wv, wq, cq, ck, cv, co)
+    wo_copies = [pltpu.make_async_copy(wo.at[:, h], wo_buf.at[h], wo_sem.at[h]) for h in range(hx)]
     w_copies = [pltpu.make_async_copy(w, w_buf.at[n], w_sem.at[n]) for n, w in enumerate(weights)]
+    a_in = pltpu.make_async_copy(a_hbm, a_ref, out_sem.at[D.parts])
+    a_in.start()
     for n in (0, 2):
         w_copies[n].start()
 
@@ -115,8 +118,9 @@
         pl.semaphore_signal(bar, inc=1, device_id=to, device_id_type=MESH)
 
     def x_core(k):
-        g = lax.rem(x * 2 + c + k, 2 * nx)
-        return g // 2, lax.rem(g, 2)
+        xo = lax.rem(x + turn((k - 1) // 2, nx), nx)
+        side = lax.rem(k - 1, 2) + jnp.where(k == 2 * nx - 1, 1, 0)
+        return xo, lax.rem(c + side, 2)
 
     def greet_x(k):
         xo, co_ = x_core(k)
@@ -126,6 +130,7 @@
     loop(1, ny, lambda k: greet(dev(z, lax.rem(y + k, ny), c, x)))
     loop(1, nz, lambda k: greet(dev(lax.rem(z + k, nz), y, c, x)))
 
+    a_in.wait()
     def norm_rows(s):
         xn[block(s, D.sites), :] = normed(a_ref[s].astype(F32), g1_ref[...].reshape(1, WIDTH))
 
@@ -161,7 +166,7 @@
                 self.src = lambda g: qkv_s.at[2, h, g, pl.ds(r * D.psites, D.psites), :]
 
         def copy(self, k):
-            xo = lax.rem(x + k, nx)
+            xo = lax.rem(x + turn(k - 1, nx), nx)
             return remote(
                 self.src(xo), self.dst, x_ss.at[self.sem], x_rs.at[self.sem], dev(z, y, c, xo)
             )
@@ -194,7 +199,7 @@
         l_own[r, h] = own * scale
 
     def y_copy(r, h, k):
-        yo = lax.rem(y + k, ny)
+        yo = lax.rem(y + turn(k - 1, ny), ny)
         return remote(
             y_send.at[r, h, block(yo, D.yrows), :],
             y_recv.at[r, h, y],
@@ -275,7 +280,7 @@
     py_rows = block(c * ny + y, D.yrows)
 
     def py_copy(r, h, k):
-        yo = lax.rem(y + k, ny)
+        yo = lax.rem(y + turn(k - 1, ny), ny)
         place = p_full.at[r, h, py_rows, :]
         return remote(place, place, py_ss.at[r, h], py_rs.at[r, h], dev(z, yo, c, x))
 
@@ -299,7 +304,7 @@
         xo, co_ = x_core(k)
         return remote(
             o_send.at[r, h, o_rows(xo, co_), :],
-            m_recv.at[r, c, x * hx + h],
+            m_recv.at[r, c, h, x],
             o_ss.at[r, h],
             o_rs.at[r, h],
             dev(z, y, co_, xo),
@@ -307,7 +312,7 @@
 
     def o_local(r, h):
         return pltpu.make_async_copy(
-            o_send.at[r, h, o_rows(x, c), :], m_recv.at[r, c, x * hx + h], o_ls.at[r, h]
+            o_send.at[r, h, o_rows(x, c), :], m_recv.at[r, c, h, x], o_ls.at[r, h]
         )
 
     def attend(r, h):
@@ -368,32 +373,37 @@
             copies.append((keep, swap))
         return copies
 
+    def mixing(r, h):
+        o_local(r, h).wait()
+        drain(o_send.at[r, h, pl.ds(0, (2 * nx - 1) * D.csites), :], o_ss.at[r, h], o_rs.at[r, h])
+        chains = [(cc, s) for cc in range(2) for s in range(D.chains)]
+        for n, (cc, s) in enumerate(chains):
+            mix[n * D.csites : (n + 1) * D.csites, :] = jnp.concatenate(
+                [m_recv[r, cc, h, g, :, s * HEAD : (s + 1) * HEAD] for g in range(nx)], axis=-1
+            )
+        if h == 0:
+            for copy in a_copies[r]:
+                copy.wait()
+            for n, (cc, s) in enumerate(chains):
+                acc[r, n * D.csites : (n + 1) * D.csites, :] = a_res[r, cc, s].astype(F32)
+
+        def columns(cb):
+            cols = block(cb, 256)
+            part = wo_buf[h, :, :, cols].reshape(nx * HEAD, 256)
+            total = acc[r, :, cols] + jnp.dot(mix[...], part, preferred_element_type=F32)
+            if h < hx - 1:
+                acc[r, :, cols] = total
+            else:
+                for n in range(D.pair):
+                    for j in range(2):
+                        c_f32[cb * 2 + j, pl.ds(n, D.csites, stride=D.pair), :] = total[
+                            n * D.csites : (n + 1) * D.csites, j * LANES : (j + 1) * LANES
+                        ]
+
+        loop(0, WIDTH // 256, columns)
+
     def after_row(r):
-        for h in range(hx):
-            o_local(r, h).wait()
-            drain(o_send.at[r, h, pl.ds(0, (2 * nx - 1) * D.csites), :], o_ss.at[r, h], o_rs.at[r, h])
-        for copy in a_copies[r]:
-            copy.wait()
-        for cc in range(2):
-            for s in range(D.chains):
-                n = cc * D.chains + s
-                mix[n * D.csites : (n + 1) * D.csites, :] = jnp.concatenate(
-                    [m_recv[r, cc, h, :, s * HEAD : (s + 1) * HEAD] for h in range(HEADS)], axis=-1
-                )
-
-        def mixing(cb):
-            cols = block(cb, 256)
-            inc = jnp.dot(mix[...], w_buf[3, :, cols], preferred_element_type=F32)
-            for cc in range(2):
-                for s in range(D.chains):
-                    n = cc * D.chains + s
-                    after = a_res[r, cc, s, :, cols].astype(F32) + inc[n * D.csites : (n + 1) * D.csites]
-                    for j in range(2):
-                        c_f32[cb * 2 + j, pl.ds(n, D.csites, stride=D.pair), :] = after[
-                            :, j * LANES : (j + 1) * LANES
-                        ]
-
-        loop(0, WIDTH // 256, mixing)
+        mixing(r, hx - 1)
         c_send[r] = pack([c_f32[j] for j in range(SLABS)])
         d_start(r, *into)
 
@@ -406,7 +416,7 @@
         wide_buf[...] = wide
         cn[...] = normed(wide, g2_ref[...].reshape(1, WIDTH))
         for m in range(3):
-            c_qkv[m] = jnp.dot(cn[...], w_buf[4 + m], preferred_element_type=F32).astype(BF)
+            c_qkv[m] = jnp.dot(cn[...], w_buf[3 + m], preferred_element_type=F32).astype(BF)
 
         def two_heads(p):
             cols = block(p, 2 * HEAD)
@@ -424,13 +434,16 @@
             c_mix[:, cols] = mixed.astype(BF)
 
         loop(0, HEADS // 2, two_heads)
-        change = jnp.dot(c_mix[...], w_buf[7], preferred_element_type=F32)
+        change = jnp.dot(c_mix[...], w_buf[6], preferred_element_type=F32)
         total = wide_buf[...] + change
         r_send[r] = pack([total[:, j * LANES : (j + 1) * LANES] for j in range(SLABS)])
         d_start(r, *back)
 
     def f_copy(r):
         return remote(f_send.at[r], out_ref.at[:, a_rows(r, c), :], f_ss.at[r], f_rs.at[r], sibling)
+
+    def out_copy(r):
+        return pltpu.make_async_copy(out_v.at[r], out_ref.at[:, a_rows(r, c), :], out_sem.at[r])
 
     def finish(r):
         d_wait(r, *back)
@@ -446,12 +459,15 @@
             f_send[r, s] = chain_rows(other * D.chains + s)
         f_copy(r).start()
         for s in range(D.chains):
-            out_ref[s, a_rows(r, c), :] = chain_rows(c * D.chains + s)
+            out_v[r, s] = chain_rows(c * D.chains + s)
+        out_copy(r).start()
 
     for m in (0, 2):
         w_copies[m].wait()
-    for n in (1, 3, 4, 5, 6, 7):
+    for n in (1, 3, 4, 5, 6):
         w_copies[n].start()
+    for copy in wo_copies:
+        copy.start()
 
     def first(h):
         Cross(0, h).start()
@@ -478,8 +494,10 @@
         Cross(1, h).start()
 
     def weights_in():
-        for n in range(3, 8):
+        for n in range(3, 7):
             w_copies[n].wait()
+        for copy in wo_copies:
+            copy.wait()
 
     plan = (
         (logits, 0, 0), (first, 2), (core_sum, 0, 0), (logits, 0, 1), (queries, 0), (queries, 1), (queries, 2),
@@ -487,15 +505,16 @@
         (core_sum, 0, 2), (y_sum, 0, 1), (z_softmax, 0, 0), (logits, 1, 0), (core_sum, 1, 0), (y_sum, 0, 2),
         (z_softmax, 0, 1), (gather_z, 0, 0), (logits, 1, 1), (core_sum, 1, 1), (y_sum, 1, 0), (z_softmax, 0, 2),
         (gather_z, 0, 1), (gather_y, 0, 0), (logits, 1, 2), (core_sum, 1, 2), (y_sum, 1, 1), (attend, 0, 0),
-        (z_softmax, 1, 0), (gather_z, 0, 2), (gather_y, 0, 1), (y_sum, 1, 2), (attend, 0, 1), (z_softmax, 1, 1),
-        (gather_z, 1, 0), (gather_y, 0, 2), (weights_in,), (attend, 0, 2), (z_softmax, 1, 2), (gather_z, 1, 1),
+        (z_softmax, 1, 0), (gather_z, 0, 2), (gather_y, 0, 1), (y_sum, 1, 2), (attend, 0, 1), (z_softmax, 1, 1), (weights_in,), (mixing, 0, 0),
+        (gather_z, 1, 0), (gather_y, 0, 2), (attend, 0, 2), (z_softmax, 1, 2), (mixing, 0, 1), (gather_z, 1, 1),
         (gather_y, 1, 0), (attend, 1, 0), (gather_z, 1, 2), (after_row, 0), (gather_y, 1, 1), (attend, 1, 1),
-        (gather_y, 1, 2), (attend, 1, 2), (after_row, 1), (column, 0), (column, 1), (finish, 0), (finish, 1),
+        (mixing, 1, 0), (gather_y, 1, 2), (attend, 1, 2), (mixing, 1, 1), (after_row, 1), (column, 0), (column, 1), (finish, 0), (finish, 1),
     )
     for step, *args in plan:
         step(*args)
-    f_copy(0).wait()
-    f_copy(1).wait()
+    for r in range(D.parts):
+        f_copy(r).wait()
+        out_copy(r).wait()
 
 
 def on_device(D, a, g1, wq, wk, wv, wo, g2, cq, ck, cv, co):
@@ -506,7 +525,9 @@
     f32 = lambda *shape: pltpu.VMEM(shape, F32)
     sem = lambda *shape: pltpu.SemaphoreType.DMA(shape)
     scratch = dict(
-        w_buf=bf(8, WIDTH, WIDTH),
+        a_ref=bf(D.chains, D.sites, WIDTH),
+        out_v=bf(N, D.chains, D.csites, WIDTH),
+        w_buf=bf(7, WIDTH, WIDTH),
         xn=bf(D.rows, WIDTH),
         qkv_s=bf(3, D.hx, D.nx, D.sites, L),
         kv_r=bf(2, H, sites, L),
@@ -522,9 +543,11 @@
         p_z=bf(N, H, D.yrows * sites // LANES, LANES),
         p_full=bf(N, H, D.prows, sites),
         o_send=bf(N, H, D.prows, L),
-        m_recv=bf(N, 2, HEADS, D.csites, L),
+        m_recv=bf(N, 2, H, D.nx, D.csites, L),
+        wo_buf=bf(H, D.nx, HEAD, WIDTH),
+        acc=f32(N, D.col_len, WIDTH),
         a_res=bf(N, 2, D.chains, D.csites, WIDTH),
-        mix=bf(D.pair * D.csites, WIDTH),
+        mix=bf(D.pair * D.csites, L),
         c_f32=f32(SLABS, D.col_len, LANES),
         c_send=bf(N, 2 * D.col_len, WIDTH // 2),
         c_recv=bf(N, 2 * D.col_len, WIDTH // 2),
@@ -535,28 +558,28 @@
         r_send=bf(N, 2 * D.col_len, WIDTH // 2),
         r_recv=bf(N, 2 * D.col_len, WIDTH // 2),
         f_send=bf(N, D.chains, D.csites, WIDTH),
-        w_sem=sem(8),
+        w_sem=sem(7), wo_sem=sem(H),
         x_ss=sem((2 + N) * H), x_rs=sem((2 + N) * H), x_ls=sem((2 + N) * H),
         a_ls=sem(N), a_ss=sem(N), a_rs=sem(N),
         c_ss=sem(N, H), c_rs=sem(N, H), y_ss=sem(N, H), y_rs=sem(N, H), z_ss=sem(N, H), z_rs=sem(N, H),
         pz_ss=sem(N, H), pz_rs=sem(N, H), py_ss=sem(N, H), py_rs=sem(N, H), pc_ss=sem(N, H), pc_rs=sem(N, H),
         o_ss=sem(N, H), o_rs=sem(N, H), o_ls=sem(N, H),
         i_ss=sem(N), i_rs=sem(N), i_ls=sem(N), b_ss=sem(N), b_rs=sem(N), b_ls=sem(N),
-        f_ss=sem(N), f_rs=sem(N),
+        f_ss=sem(N), f_rs=sem(N), out_sem=sem(N + 1),
     )
     flops = 2 * (8 * D.rows * WIDTH * WIDTH + 2 * D.hx * sites * sites * L)
     return pl.pallas_call(
         functools.partial(layer, D),
         out_shape=jax.ShapeDtypeStruct(a.shape, a.dtype),
-        in_specs=[vmem] * 3 + [hbm] * 8,
-        out_specs=vmem,
+        in_specs=[hbm] + [vmem] * 2 + [hbm] * 8,
+        out_specs=hbm,
         scratch_shapes=list(scratch.values()),
         compiler_params=pltpu.CompilerParams(
             collective_id=0, has_side_effects=True, vmem_limit_bytes=60 * 2**20
         ),
         cost_estimate=pl.CostEstimate(flops=flops, bytes_accessed=12 * 2**20, transcendentals=2**21),
         name="msa_layer",
-    )(a, g1, g2, wq, wk, wv, wo, cq, ck, cv, co)
+    )(a, g1, g2, wq, wk, wv, wo.reshape(D.nx, H, HEAD, WIDTH), cq, ck, cv, co)
 
 
 def solution(mesh):

time: 100 us -> 98 us (0.980)
  Pallas kernels: 98.2 us -> 95.8 us
    pallas_call x1, Pallas kernels: 98.2 us -> 95.8 us  [on_device(): pl.pallas_call(functools.partial(layer, D), out_shape=jax.ShapeDtypeStruc...]
where the time goes in v5:
time: 98 us; the launch traced here: 97.9 us
  Pallas kernels  95.8 us (98%)
  local copies, waits for them, and re-layouts  2.06 us (2%)
    pallas_call x1, Pallas kernels, on_device(): pl.pallas_call(functools.partial(layer, D), out_shape=jax.ShapeDtypeStruc...  95.8 us
    unnamed x1, local copies, waits for them, and re-layouts  2.06 us

profile of v5, /device:TPU:1, one launch (start us, length us, event | category | flops | bytes accessed | tf_op | source)
XLA Modules:
  0.0 97.9 jit_solution(8425852249730373367)
XLA Ops:
  0.0 95.8 %msa_layer.1 = bf16[4,128,768]{2,1,0:T(8,128)(2,1)} custom-call(bf16[4,128,768]{2,1,0:T(8,128)(2,1)} %a_hbm.1, f32[768]{0:T(1024)} %g1_ref.1, f32[768]{0:T(1024)} %g2_ref.1, bf16[768,768]{1,0:T(8,128)(2,1)} %wq.1, bf16[768,768]{1,0:T(8,128)(2,1)} %wk.1, bf16[768,768]{1,0:T(8,128)(2,1)} %wv.1, bf16[4,3,64,768]{3,2,1,0:T(8,128)(2,1)} %bitcast.1, ...), custom_call_target="tpu_custom_call" | custom-call | flops 5637144576 | bytes 12582912 | tf_op jit(solution)/shard_map/msa_layer/pallas_call | solution.py:571
  95.8 2.1 %copy.13 = bf16[4,128,768]{2,1,0:T(8,128)(2,1)} copy(bf16[4,128,768]{2,1,0:T(8,128)(2,1)} %msa_layer.1) | data formatting | bytes 1572864

commit v6 on v5

--- a/solution.py
+++ b/solution.py
@@ -502,13 +502,14 @@
     plan = (
         (logits, 0, 0), (first, 2), (core_sum, 0, 0), (logits, 0, 1), (queries, 0), (queries, 1), (queries, 2),
         (core_sum, 0, 1), (y_sum, 0, 0), (logits, 0, 2), (values, 0), (values, 1), (values, 2),
-        (core_sum, 0, 2), (y_sum, 0, 1), (z_softmax, 0, 0), (logits, 1, 0), (core_sum, 1, 0), (y_sum, 0, 2),
-        (z_softmax, 0, 1), (gather_z, 0, 0), (logits, 1, 1), (core_sum, 1, 1), (y_sum, 1, 0), (z_softmax, 0, 2),
-        (gather_z, 0, 1), (gather_y, 0, 0), (logits, 1, 2), (core_sum, 1, 2), (y_sum, 1, 1), (attend, 0, 0),
-        (z_softmax, 1, 0), (gather_z, 0, 2), (gather_y, 0, 1), (y_sum, 1, 2), (attend, 0, 1), (z_softmax, 1, 1), (weights_in,), (mixing, 0, 0),
-        (gather_z, 1, 0), (gather_y, 0, 2), (attend, 0, 2), (z_softmax, 1, 2), (mixing, 0, 1), (gather_z, 1, 1),
-        (gather_y, 1, 0), (attend, 1, 0), (gather_z, 1, 2), (after_row, 0), (gather_y, 1, 1), (attend, 1, 1),
-        (mixing, 1, 0), (gather_y, 1, 2), (attend, 1, 2), (mixing, 1, 1), (after_row, 1), (column, 0), (column, 1), (finish, 0), (finish, 1),
+        (core_sum, 0, 2), (y_sum, 0, 1), (logits, 1, 0), (z_softmax, 0, 0), (core_sum, 1, 0), (logits, 1, 1),
+        (core_sum, 1, 1), (logits, 1, 2), (core_sum, 1, 2), (y_sum, 0, 2), (z_softmax, 0, 1), (gather_z, 0, 0),
+        (y_sum, 1, 0), (y_sum, 1, 1), (y_sum, 1, 2), (z_softmax, 0, 2), (gather_z, 0, 1), (gather_y, 0, 0),
+        (z_softmax, 1, 0), (attend, 0, 0), (z_softmax, 1, 1), (z_softmax, 1, 2), (gather_z, 0, 2),
+        (gather_y, 0, 1), (attend, 0, 1), (gather_z, 1, 0), (gather_z, 1, 1), (weights_in,), (mixing, 0, 0),
+        (gather_z, 1, 2), (gather_y, 0, 2), (attend, 0, 2), (gather_y, 1, 0), (attend, 1, 0), (mixing, 0, 1),
+        (gather_y, 1, 1), (attend, 1, 1), (after_row, 0), (gather_y, 1, 2), (attend, 1, 2), (mixing, 1, 0),
+        (mixing, 1, 1), (after_row, 1), (column, 0), (column, 1), (finish, 0), (finish, 1),
     )
     for step, *args in plan:
         step(*args)

time: 98 us -> 96.9 us (0.989)
  Pallas kernels: 95.8 us -> 94.7 us
    pallas_call x1, Pallas kernels: 95.8 us -> 94.7 us  [on_device(): pl.pallas_call(functools.partial(layer, D), out_shape=jax.ShapeDtypeStruc...]
where the time goes in v6:
time: 96.9 us; the launch traced here: 96.7 us
  Pallas kernels  94.7 us (98%)
  local copies, waits for them, and re-layouts  2.06 us (2%)
    pallas_call x1, Pallas kernels, on_device(): pl.pallas_call(functools.partial(layer, D), out_shape=jax.ShapeDtypeStruc...  94.7 us
    unnamed x1, local copies, waits for them, and re-layouts  2.06 us

profile of v6, /device:TPU:1, one launch (start us, length us, event | category | flops | bytes accessed | tf_op | source)
XLA Modules:
  0.0 96.7 jit_solution(61176162290282850)
XLA Ops:
  0.0 94.7 %msa_layer.1 = bf16[4,128,768]{2,1,0:T(8,128)(2,1)} custom-call(bf16[4,128,768]{2,1,0:T(8,128)(2,1)} %a_hbm.1, f32[768]{0:T(1024)} %g1_ref.1, f32[768]{0:T(1024)} %g2_ref.1, bf16[768,768]{1,0:T(8,128)(2,1)} %wq.1, bf16[768,768]{1,0:T(8,128)(2,1)} %wk.1, bf16[768,768]{1,0:T(8,128)(2,1)} %wv.1, bf16[4,3,64,768]{3,2,1,0:T(8,128)(2,1)} %bitcast.1, ...), custom_call_target="tpu_custom_call" | custom-call | flops 5637144576 | bytes 12582912 | tf_op jit(solution)/shard_map/msa_layer/pallas_call | solution.py:572
  94.7 2.1 %copy.13 = bf16[4,128,768]{2,1,0:T(8,128)(2,1)} copy(bf16[4,128,768]{2,1,0:T(8,128)(2,1)} %msa_layer.1) | data formatting | bytes 1572864

commit v7 on v6

--- a/solution.py
+++ b/solution.py
@@ -508,7 +508,7 @@
         (z_softmax, 1, 0), (attend, 0, 0), (z_softmax, 1, 1), (z_softmax, 1, 2), (gather_z, 0, 2),
         (gather_y, 0, 1), (attend, 0, 1), (gather_z, 1, 0), (gather_z, 1, 1), (weights_in,), (mixing, 0, 0),
         (gather_z, 1, 2), (gather_y, 0, 2), (attend, 0, 2), (gather_y, 1, 0), (attend, 1, 0), (mixing, 0, 1),
-        (gather_y, 1, 1), (attend, 1, 1), (after_row, 0), (gather_y, 1, 2), (attend, 1, 2), (mixing, 1, 0),
+        (gather_y, 1, 1), (attend, 1, 1), (mixing, 1, 0), (after_row, 0), (gather_y, 1, 2), (attend, 1, 2),
         (mixing, 1, 1), (after_row, 1), (column, 0), (column, 1), (finish, 0), (finish, 1),
     )
     for step, *args in plan:

time: 96.9 us -> 99.2 us (1.024)
  Pallas kernels: 94.7 us -> 97 us
    pallas_call x1, Pallas kernels: 94.7 us -> 97 us  [on_device(): pl.pallas_call(functools.partial(layer, D), out_shape=jax.ShapeDtypeStruc...]
where the time goes in v7:
time: 99.2 us; the launch traced here: 99.1 us
  Pallas kernels  97 us (98%)
  local copies, waits for them, and re-layouts  2.06 us (2%)
    pallas_call x1, Pallas kernels, on_device(): pl.pallas_call(functools.partial(layer, D), out_shape=jax.ShapeDtypeStruc...  97 us
    unnamed x1, local copies, waits for them, and re-layouts  2.06 us

profile of v7, /device:TPU:1, one launch (start us, length us, event | category | flops | bytes accessed | tf_op | source)
XLA Modules:
  0.0 99.1 jit_solution(11911101786196570564)
XLA Ops:
  0.0 97.0 %msa_layer.1 = bf16[4,128,768]{2,1,0:T(8,128)(2,1)} custom-call(bf16[4,128,768]{2,1,0:T(8,128)(2,1)} %a_hbm.1, f32[768]{0:T(1024)} %g1_ref.1, f32[768]{0:T(1024)} %g2_ref.1, bf16[768,768]{1,0:T(8,128)(2,1)} %wq.1, bf16[768,768]{1,0:T(8,128)(2,1)} %wk.1, bf16[768,768]{1,0:T(8,128)(2,1)} %wv.1, bf16[4,3,64,768]{3,2,1,0:T(8,128)(2,1)} %bitcast.1, ...), custom_call_target="tpu_custom_call" | custom-call | flops 5637144576 | bytes 12582912 | tf_op jit(solution)/shard_map/msa_layer/pallas_call | solution.py:572
  97.0 2.1 %copy.13 = bf16[4,128,768]{2,1,0:T(8,128)(2,1)} copy(bf16[4,128,768]{2,1,0:T(8,128)(2,1)} %msa_layer.1) | data formatting | bytes 1572864
